TPU v7x, 128 devices: a whole 4x4x4 slice. The times are simulated.
128 devices in a mesh: dp: 32 (over z_hi, y, x), tensor: 4 (over z_lo, core).
Axes of the slice: x: 4, y: 4, z: 4 (z_hi: 2, z_lo: 2; z = z_hi * 2 + z_lo), core: 2. Of those that a mesh axis runs over, the one named last changes fastest.
Arguments:
- train_act: bfloat16 [128, 128, 5120], P('dp', None, 'tensor'), may hold values from -6 to 6
- train_grad: bfloat16 [128, 128, 5120], P('dp', None, 'tensor'), may hold values from -6 to 6
- val_act: bfloat16 [32, 128, 5120], P('dp', None, 'tensor'), may hold values from -6 to 6
- val_grad: bfloat16 [32, 128, 5120], P('dp', None, 'tensor'), may hold values from -6 to 6
Outputs:
- shapley: float32 [128, 32], P('dp')
All inputs are finite; a program needn't handle non-finite values.
Results may differ from a plain program's by a relative error of at most 0.0003.
Values may be sent and summed in bfloat16 or wider, within the bound.
A program may use at most 64 MiB of HBM per device.

v0:
```python
import jax
import jax.numpy as jnp
from jax import lax
from jax.sharding import PartitionSpec as P

D = 5120


def passed_along(value, axis, steps):
    count = lax.axis_size(axis)
    pairs = [(source, (source + steps) % count) for source in range(count)]
    return lax.ppermute(value, axis, pairs)


def per_device(train_act, train_grad, val_act, val_grad):
    ndevices = lax.axis_size("dp")
    myself = lax.axis_index("dp")
    scale = D ** (-0.5)
    seq_len = train_act.shape[1]
    columns = jnp.arange(ndevices, dtype=jnp.int32)

    def pair_terms(block_act, block_grad):
        part_act = (
            jnp.einsum("ntd,sd->nts", train_act, block_act, preferred_element_type=jnp.float32)
            * scale
        )
        part_grad = (
            jnp.einsum("ntd,sd->nts", train_grad, block_grad, preferred_element_type=jnp.float32)
            * scale
        )
        act_gram, grad_gram = (
            lax.psum_scatter(part_act, "tensor", scatter_dimension=1, tiled=True),
            lax.psum_scatter(part_grad, "tensor", scatter_dimension=1, tiled=True),
        )
        return jnp.sum(act_gram * grad_gram, axis=1)

    def place(scores, column, values):
        onehot = (columns == column).astype(jnp.float32)
        return scores + values[:, None] * onehot[None, :]

    scores = jnp.zeros((train_act.shape[0], ndevices), jnp.float32)

    def accumulate(step, scores, held_act, held_grad):
        terms = pair_terms(held_act, held_grad)
        column = jnp.mod(myself - step, ndevices)
        return place(scores, column, jnp.sum(terms, axis=1))

    def advance(step, carry):
        scores, held_act, held_grad = carry
        scores = accumulate(step, scores, held_act, held_grad)
        held_act, held_grad = passed_along((held_act, held_grad), "dp", 1)
        return (scores, held_act, held_grad)

    scores, held_act, held_grad = lax.fori_loop(
        0, ndevices - 1, advance, (scores, val_act[0], val_grad[0])
    )
    scores = accumulate(ndevices - 1, scores, held_act, held_grad)
    total = lax.psum(scores, "tensor")
    return total / seq_len


def solution(mesh):
    placed = (
        P("dp", None, "tensor"),
        P("dp", None, "tensor"),
        P("dp", None, "tensor"),
        P("dp", None, "tensor"),
    )
    return jax.shard_map(
        per_device, mesh=mesh, in_specs=placed, out_specs=P("dp", None), check_vma=False
    )
```

profile of v0, /device:TPU:1, one launch (start us, length us, event | category | flops | bytes accessed | tf_op | source)
XLA Modules:
  0.0 1585.2 jit_solution(4308434212226109729)
XLA Ops:
  9.4 1520.2 %while.20 = (s32[]{:T(128)}, f32[4,32]{1,0:T(4,128)S(1)}, bf16[128,1280]{1,0:T(8,128)(2,1)S(1)}, bf16[128,1280]{1,0:T(8,128)(2,1)S(1)}, bf16[4,128,1280]{2,1,0:T...) while((s32[]{:T(128)}, f32[4,32]{1,0:T(4,128)S(1)}, ...), condition=%wide.region_4.5_spmd.clone, body=%wide.region_0.4_spmd.clone.sunk | while | flops 335708608 | bytes 9832116 | solution.py:54
  16.6 28.2 %reduce-scatter.3.cloned.1.call-done = f32[4,32,128]{2,1,0:T(8,128)} async-done(((f32[4,128,128]{2,1,0:T(8,128)}), f32[4,32,128]{2,1,0:T(8,128)}) %reduce-scatter.3.cloned.1.call-update) | async-done | bytes 65552 | tf_op jit(solution)/shard_map/while/body/eval_jaxpr/reduce_scatter | solution.py:32
  66.9 26.6 %reduce-scatter.3.cloned.1.call-done = f32[4,32,128]{2,1,0:T(8,128)} async-done(((f32[4,128,128]{2,1,0:T(8,128)}), f32[4,32,128]{2,1,0:T(8,128)}) %reduce-scatter.3.cloned.1.call-update) | async-done | bytes 65552 | tf_op jit(solution)/shard_map/while/body/eval_jaxpr/reduce_scatter | solution.py:32
  115.8 26.6 %reduce-scatter.3.cloned.1.call-done = f32[4,32,128]{2,1,0:T(8,128)} async-done(((f32[4,128,128]{2,1,0:T(8,128)}), f32[4,32,128]{2,1,0:T(8,128)}) %reduce-scatter.3.cloned.1.call-update) | async-done | bytes 65552 | tf_op jit(solution)/shard_map/while/body/eval_jaxpr/reduce_scatter | solution.py:32
  164.7 26.6 %reduce-scatter.3.cloned.1.call-done = f32[4,32,128]{2,1,0:T(8,128)} async-done(((f32[4,128,128]{2,1,0:T(8,128)}), f32[4,32,128]{2,1,0:T(8,128)}) %reduce-scatter.3.cloned.1.call-update) | async-done | bytes 65552 | tf_op jit(solution)/shard_map/while/body/eval_jaxpr/reduce_scatter | solution.py:32
  191.3 15.0 reduce-scatter.5.cloned.1.call-done
  213.8 26.6 %reduce-scatter.3.cloned.1.call-done = f32[4,32,128]{2,1,0:T(8,128)} async-done(((f32[4,128,128]{2,1,0:T(8,128)}), f32[4,32,128]{2,1,0:T(8,128)}) %reduce-scatter.3.cloned.1.call-update) | async-done | bytes 65552 | tf_op jit(solution)/shard_map/while/body/eval_jaxpr/reduce_scatter | solution.py:32
  262.6 26.6 %reduce-scatter.3.cloned.1.call-done = f32[4,32,128]{2,1,0:T(8,128)} async-done(((f32[4,128,128]{2,1,0:T(8,128)}), f32[4,32,128]{2,1,0:T(8,128)}) %reduce-scatter.3.cloned.1.call-update) | async-done | bytes 65552 | tf_op jit(solution)/shard_map/while/body/eval_jaxpr/reduce_scatter | solution.py:32
  311.5 26.6 %reduce-scatter.3.cloned.1.call-done = f32[4,32,128]{2,1,0:T(8,128)} async-done(((f32[4,128,128]{2,1,0:T(8,128)}), f32[4,32,128]{2,1,0:T(8,128)}) %reduce-scatter.3.cloned.1.call-update) | async-done | bytes 65552 | tf_op jit(solution)/shard_map/while/body/eval_jaxpr/reduce_scatter | solution.py:32
  360.4 26.6 %reduce-scatter.3.cloned.1.call-done = f32[4,32,128]{2,1,0:T(8,128)} async-done(((f32[4,128,128]{2,1,0:T(8,128)}), f32[4,32,128]{2,1,0:T(8,128)}) %reduce-scatter.3.cloned.1.call-update) | async-done | bytes 65552 | tf_op jit(solution)/shard_map/while/body/eval_jaxpr/reduce_scatter | solution.py:32
  409.3 26.6 %reduce-scatter.3.cloned.1.call-done = f32[4,32,128]{2,1,0:T(8,128)} async-done(((f32[4,128,128]{2,1,0:T(8,128)}), f32[4,32,128]{2,1,0:T(8,128)}) %reduce-scatter.3.cloned.1.call-update) | async-done | bytes 65552 | tf_op jit(solution)/shard_map/while/body/eval_jaxpr/reduce_scatter | solution.py:32
  458.2 26.6 %reduce-scatter.3.cloned.1.call-done = f32[4,32,128]{2,1,0:T(8,128)} async-done(((f32[4,128,128]{2,1,0:T(8,128)}), f32[4,32,128]{2,1,0:T(8,128)}) %reduce-scatter.3.cloned.1.call-update) | async-done | bytes 65552 | tf_op jit(solution)/shard_map/while/body/eval_jaxpr/reduce_scatter | solution.py:32
  507.1 26.6 %reduce-scatter.3.cloned.1.call-done = f32[4,32,128]{2,1,0:T(8,128)} async-done(((f32[4,128,128]{2,1,0:T(8,128)}), f32[4,32,128]{2,1,0:T(8,128)}) %reduce-scatter.3.cloned.1.call-update) | async-done | bytes 65552 | tf_op jit(solution)/shard_map/while/body/eval_jaxpr/reduce_scatter | solution.py:32
  556.2 26.6 %reduce-scatter.3.cloned.1.call-done = f32[4,32,128]{2,1,0:T(8,128)} async-done(((f32[4,128,128]{2,1,0:T(8,128)}), f32[4,32,128]{2,1,0:T(8,128)}) %reduce-scatter.3.cloned.1.call-update) | async-done | bytes 65552 | tf_op jit(solution)/shard_map/while/body/eval_jaxpr/reduce_scatter | solution.py:32
  605.1 26.6 %reduce-scatter.3.cloned.1.call-done = f32[4,32,128]{2,1,0:T(8,128)} async-done(((f32[4,128,128]{2,1,0:T(8,128)}), f32[4,32,128]{2,1,0:T(8,128)}) %reduce-scatter.3.cloned.1.call-update) | async-done | bytes 65552 | tf_op jit(solution)/shard_map/while/body/eval_jaxpr/reduce_scatter | solution.py:32
  654.0 26.6 %reduce-scatter.3.cloned.1.call-done = f32[4,32,128]{2,1,0:T(8,128)} async-done(((f32[4,128,128]{2,1,0:T(8,128)}), f32[4,32,128]{2,1,0:T(8,128)}) %reduce-scatter.3.cloned.1.call-update) | async-done | bytes 65552 | tf_op jit(solution)/shard_map/while/body/eval_jaxpr/reduce_scatter | solution.py:32
  703.0 26.6 %reduce-scatter.3.cloned.1.call-done = f32[4,32,128]{2,1,0:T(8,128)} async-done(((f32[4,128,128]{2,1,0:T(8,128)}), f32[4,32,128]{2,1,0:T(8,128)}) %reduce-scatter.3.cloned.1.call-update) | async-done | bytes 65552 | tf_op jit(solution)/shard_map/while/body/eval_jaxpr/reduce_scatter | solution.py:32
  751.9 26.6 %reduce-scatter.3.cloned.1.call-done = f32[4,32,128]{2,1,0:T(8,128)} async-done(((f32[4,128,128]{2,1,0:T(8,128)}), f32[4,32,128]{2,1,0:T(8,128)}) %reduce-scatter.3.cloned.1.call-update) | async-done | bytes 65552 | tf_op jit(solution)/shard_map/while/body/eval_jaxpr/reduce_scatter | solution.py:32
  778.5 15.0 reduce-scatter.5.cloned.1.call-done
  800.9 26.6 %reduce-scatter.3.cloned.1.call-done = f32[4,32,128]{2,1,0:T(8,128)} async-done(((f32[4,128,128]{2,1,0:T(8,128)}), f32[4,32,128]{2,1,0:T(8,128)}) %reduce-scatter.3.cloned.1.call-update) | async-done | bytes 65552 | tf_op jit(solution)/shard_map/while/body/eval_jaxpr/reduce_scatter | solution.py:32
  827.6 15.0 reduce-scatter.5.cloned.1.call-done
  850.0 26.6 %reduce-scatter.3.cloned.1.call-done = f32[4,32,128]{2,1,0:T(8,128)} async-done(((f32[4,128,128]{2,1,0:T(8,128)}), f32[4,32,128]{2,1,0:T(8,128)}) %reduce-scatter.3.cloned.1.call-update) | async-done | bytes 65552 | tf_op jit(solution)/shard_map/while/body/eval_jaxpr/reduce_scatter | solution.py:32
  898.9 26.6 %reduce-scatter.3.cloned.1.call-done = f32[4,32,128]{2,1,0:T(8,128)} async-done(((f32[4,128,128]{2,1,0:T(8,128)}), f32[4,32,128]{2,1,0:T(8,128)}) %reduce-scatter.3.cloned.1.call-update) | async-done | bytes 65552 | tf_op jit(solution)/shard_map/while/body/eval_jaxpr/reduce_scatter | solution.py:32
  925.5 15.0 reduce-scatter.5.cloned.1.call-done
  947.9 26.4 %reduce-scatter.3.cloned.1.call-done = f32[4,32,128]{2,1,0:T(8,128)} async-done(((f32[4,128,128]{2,1,0:T(8,128)}), f32[4,32,128]{2,1,0:T(8,128)}) %reduce-scatter.3.cloned.1.call-update) | async-done | bytes 65552 | tf_op jit(solution)/shard_map/while/body/eval_jaxpr/reduce_scatter | solution.py:32
  974.3 15.3 reduce-scatter.5.cloned.1.call-done
  997.0 26.6 %reduce-scatter.3.cloned.1.call-done = f32[4,32,128]{2,1,0:T(8,128)} async-done(((f32[4,128,128]{2,1,0:T(8,128)}), f32[4,32,128]{2,1,0:T(8,128)}) %reduce-scatter.3.cloned.1.call-update) | async-done | bytes 65552 | tf_op jit(solution)/shard_map/while/body/eval_jaxpr/reduce_scatter | solution.py:32
  1023.6 15.0 reduce-scatter.5.cloned.1.call-done
  1046.0 26.6 %reduce-scatter.3.cloned.1.call-done = f32[4,32,128]{2,1,0:T(8,128)} async-done(((f32[4,128,128]{2,1,0:T(8,128)}), f32[4,32,128]{2,1,0:T(8,128)}) %reduce-scatter.3.cloned.1.call-update) | async-done | bytes 65552 | tf_op jit(solution)/shard_map/while/body/eval_jaxpr/reduce_scatter | solution.py:32
  1072.6 15.0 reduce-scatter.5.cloned.1.call-done
  1095.0 26.6 %reduce-scatter.3.cloned.1.call-done = f32[4,32,128]{2,1,0:T(8,128)} async-done(((f32[4,128,128]{2,1,0:T(8,128)}), f32[4,32,128]{2,1,0:T(8,128)}) %reduce-scatter.3.cloned.1.call-update) | async-done | bytes 65552 | tf_op jit(solution)/shard_map/while/body/eval_jaxpr/reduce_scatter | solution.py:32
  1143.9 26.3 %reduce-scatter.3.cloned.1.call-done = f32[4,32,128]{2,1,0:T(8,128)} async-done(((f32[4,128,128]{2,1,0:T(8,128)}), f32[4,32,128]{2,1,0:T(8,128)}) %reduce-scatter.3.cloned.1.call-update) | async-done | bytes 65552 | tf_op jit(solution)/shard_map/while/body/eval_jaxpr/reduce_scatter | solution.py:32
  1170.3 15.1 reduce-scatter.5.cloned.1.call-done
  1192.8 26.3 %reduce-scatter.3.cloned.1.call-done = f32[4,32,128]{2,1,0:T(8,128)} async-done(((f32[4,128,128]{2,1,0:T(8,128)}), f32[4,32,128]{2,1,0:T(8,128)}) %reduce-scatter.3.cloned.1.call-update) | async-done | bytes 65552 | tf_op jit(solution)/shard_map/while/body/eval_jaxpr/reduce_scatter | solution.py:32
  1219.2 15.3 reduce-scatter.5.cloned.1.call-done
  1241.8 26.3 %reduce-scatter.3.cloned.1.call-done = f32[4,32,128]{2,1,0:T(8,128)} async-done(((f32[4,128,128]{2,1,0:T(8,128)}), f32[4,32,128]{2,1,0:T(8,128)}) %reduce-scatter.3.cloned.1.call-update) | async-done | bytes 65552 | tf_op jit(solution)/shard_map/while/body/eval_jaxpr/reduce_scatter | solution.py:32
  1268.2 15.3 reduce-scatter.5.cloned.1.call-done
  1290.9 26.3 %reduce-scatter.3.cloned.1.call-done = f32[4,32,128]{2,1,0:T(8,128)} async-done(((f32[4,128,128]{2,1,0:T(8,128)}), f32[4,32,128]{2,1,0:T(8,128)}) %reduce-scatter.3.cloned.1.call-update) | async-done | bytes 65552 | tf_op jit(solution)/shard_map/while/body/eval_jaxpr/reduce_scatter | solution.py:32
  1317.3 15.3 reduce-scatter.5.cloned.1.call-done
  1339.9 26.4 %reduce-scatter.3.cloned.1.call-done = f32[4,32,128]{2,1,0:T(8,128)} async-done(((f32[4,128,128]{2,1,0:T(8,128)}), f32[4,32,128]{2,1,0:T(8,128)}) %reduce-scatter.3.cloned.1.call-update) | async-done | bytes 65552 | tf_op jit(solution)/shard_map/while/body/eval_jaxpr/reduce_scatter | solution.py:32
  1366.3 15.3 reduce-scatter.5.cloned.1.call-done
  1389.0 26.3 %reduce-scatter.3.cloned.1.call-done = f32[4,32,128]{2,1,0:T(8,128)} async-done(((f32[4,128,128]{2,1,0:T(8,128)}), f32[4,32,128]{2,1,0:T(8,128)}) %reduce-scatter.3.cloned.1.call-update) | async-done | bytes 65552 | tf_op jit(solution)/shard_map/while/body/eval_jaxpr/reduce_scatter | solution.py:32
  1415.3 15.1 reduce-scatter.5.cloned.1.call-done
  1437.9 26.4 %reduce-scatter.3.cloned.1.call-done = f32[4,32,128]{2,1,0:T(8,128)} async-done(((f32[4,128,128]{2,1,0:T(8,128)}), f32[4,32,128]{2,1,0:T(8,128)}) %reduce-scatter.3.cloned.1.call-update) | async-done | bytes 65552 | tf_op jit(solution)/shard_map/while/body/eval_jaxpr/reduce_scatter | solution.py:32
  1464.2 15.3 reduce-scatter.5.cloned.1.call-done
  1486.9 26.4 %reduce-scatter.3.cloned.1.call-done = f32[4,32,128]{2,1,0:T(8,128)} async-done(((f32[4,128,128]{2,1,0:T(8,128)}), f32[4,32,128]{2,1,0:T(8,128)}) %reduce-scatter.3.cloned.1.call-update) | async-done | bytes 65552 | tf_op jit(solution)/shard_map/while/body/eval_jaxpr/reduce_scatter | solution.py:32
  1513.3 15.3 reduce-scatter.5.cloned.1.call-done
  1533.8 37.4 %all-reduce.5.cloned.1.call-done = (f32[4,128,128]{2,0,1:T(4,128)}, f32[4,128,128]{2,0,1:T(4,128)}) async-done(((f32[4,128,128]{2,0,1:T(4,128)}, f32[4,128,128]{2,0,1:T(4,128)}), (f32[4,128,128]{2,0,1:T(4,128)}, f32[4,128,128]{2,0,1:T(4,128)})) %all-reduce.5.cloned.1.call-update) | async-done | bytes 524304
  (502 shorter events, 479.0 us)
Async XLA Ops:
  12.0 47.5 %reduce-scatter.5.cloned.1.call-start = ((), (), s32[]{:S(2)}) async-start(), calls=%async_computation.4 | async-start | bytes 327680 | tf_op jit(solution)/shard_map/while/body/eval_jaxpr/reduce_scatter | solution.py:33
  13.3 47.3 %collective-permute-start = (bf16[128,1280]{1,0:T(8,128)(2,1)S(1)}, bf16[128,1280]{1,0:T(8,128)(2,1)S(1)}, u32[]{:S(2)}, u32[]{:S(2)}) collective-permute-start(bf16[128,1280]{1,0:T(8,128)(2,1)S(1)} %copy.13), channel_id=1, source_target_pairs={{0,4},{4,8},{8,12},{12,16},{16,20},{20,24},{24,28},{28,32},{32,36}... | collective-permute-start | bytes 983048 | tf_op jit(solution)/shard_map/while/body/eval_jaxpr/ppermute | solution.py:12
  15.4 45.2 %collective-permute-start.1 = (bf16[128,1280]{1,0:T(8,128)(2,1)S(1)}, bf16[128,1280]{1,0:T(8,128)(2,1)S(1)}, u32[]{:S(2)}, u32[]{:S(2)}) collective-permute-start(bf16[128,1280]{1,0:T(8,128)(2,1)S(1)} %copy.14), channel_id=1, source_target_pairs={{0,4},{4,8},{8,12},{12,16},{16,20},{20,24},{24,28},{28,32},{32,36}... | collective-permute-start | bytes 983048 | tf_op jit(solution)/shard_map/while/body/eval_jaxpr/ppermute | solution.py:12
  63.2 45.2 %reduce-scatter.5.cloned.1.call-start = ((), (), s32[]{:S(2)}) async-start(), calls=%async_computation.4 | async-start | bytes 327680 | tf_op jit(solution)/shard_map/while/body/eval_jaxpr/reduce_scatter | solution.py:33
  112.1 45.2 %reduce-scatter.5.cloned.1.call-start = ((), (), s32[]{:S(2)}) async-start(), calls=%async_computation.4 | async-start | bytes 327680 | tf_op jit(solution)/shard_map/while/body/eval_jaxpr/reduce_scatter | solution.py:33
  161.0 45.4 %reduce-scatter.5.cloned.1.call-start = ((), (), s32[]{:S(2)}) async-start(), calls=%async_computation.4 | async-start | bytes 327680 | tf_op jit(solution)/shard_map/while/body/eval_jaxpr/reduce_scatter | solution.py:33
  162.3 45.1 %collective-permute-start = (bf16[128,1280]{1,0:T(8,128)(2,1)S(1)}, bf16[128,1280]{1,0:T(8,128)(2,1)S(1)}, u32[]{:S(2)}, u32[]{:S(2)}) collective-permute-start(bf16[128,1280]{1,0:T(8,128)(2,1)S(1)} %copy.13), channel_id=1, source_target_pairs={{0,4},{4,8},{8,12},{12,16},{16,20},{20,24},{24,28},{28,32},{32,36}... | collective-permute-start | bytes 983048 | tf_op jit(solution)/shard_map/while/body/eval_jaxpr/ppermute | solution.py:12
  210.0 45.2 %reduce-scatter.5.cloned.1.call-start = ((), (), s32[]{:S(2)}) async-start(), calls=%async_computation.4 | async-start | bytes 327680 | tf_op jit(solution)/shard_map/while/body/eval_jaxpr/reduce_scatter | solution.py:33
  258.9 45.2 %reduce-scatter.5.cloned.1.call-start = ((), (), s32[]{:S(2)}) async-start(), calls=%async_computation.4 | async-start | bytes 327680 | tf_op jit(solution)/shard_map/while/body/eval_jaxpr/reduce_scatter | solution.py:33
  307.8 45.2 %reduce-scatter.5.cloned.1.call-start = ((), (), s32[]{:S(2)}) async-start(), calls=%async_computation.4 | async-start | bytes 327680 | tf_op jit(solution)/shard_map/while/body/eval_jaxpr/reduce_scatter | solution.py:33
  356.7 45.2 %reduce-scatter.5.cloned.1.call-start = ((), (), s32[]{:S(2)}) async-start(), calls=%async_computation.4 | async-start | bytes 327680 | tf_op jit(solution)/shard_map/while/body/eval_jaxpr/reduce_scatter | solution.py:33
  405.6 45.2 %reduce-scatter.5.cloned.1.call-start = ((), (), s32[]{:S(2)}) async-start(), calls=%async_computation.4 | async-start | bytes 327680 | tf_op jit(solution)/shard_map/while/body/eval_jaxpr/reduce_scatter | solution.py:33
  454.5 45.2 %reduce-scatter.5.cloned.1.call-start = ((), (), s32[]{:S(2)}) async-start(), calls=%async_computation.4 | async-start | bytes 327680 | tf_op jit(solution)/shard_map/while/body/eval_jaxpr/reduce_scatter | solution.py:33
  503.4 45.4 %reduce-scatter.5.cloned.1.call-start = ((), (), s32[]{:S(2)}) async-start(), calls=%async_computation.4 | async-start | bytes 327680 | tf_op jit(solution)/shard_map/while/body/eval_jaxpr/reduce_scatter | solution.py:33
  504.7 45.1 %collective-permute-start = (bf16[128,1280]{1,0:T(8,128)(2,1)S(1)}, bf16[128,1280]{1,0:T(8,128)(2,1)S(1)}, u32[]{:S(2)}, u32[]{:S(2)}) collective-permute-start(bf16[128,1280]{1,0:T(8,128)(2,1)S(1)} %copy.13), channel_id=1, source_target_pairs={{0,4},{4,8},{8,12},{12,16},{16,20},{20,24},{24,28},{28,32},{32,36}... | collective-permute-start | bytes 983048 | tf_op jit(solution)/shard_map/while/body/eval_jaxpr/ppermute | solution.py:12
  552.4 45.2 %reduce-scatter.5.cloned.1.call-start = ((), (), s32[]{:S(2)}) async-start(), calls=%async_computation.4 | async-start | bytes 327680 | tf_op jit(solution)/shard_map/while/body/eval_jaxpr/reduce_scatter | solution.py:33
  601.3 45.2 %reduce-scatter.5.cloned.1.call-start = ((), (), s32[]{:S(2)}) async-start(), calls=%async_computation.4 | async-start | bytes 327680 | tf_op jit(solution)/shard_map/while/body/eval_jaxpr/reduce_scatter | solution.py:33
  650.2 45.4 %reduce-scatter.5.cloned.1.call-start = ((), (), s32[]{:S(2)}) async-start(), calls=%async_computation.4 | async-start | bytes 327680 | tf_op jit(solution)/shard_map/while/body/eval_jaxpr/reduce_scatter | solution.py:33
  651.5 45.1 %collective-permute-start = (bf16[128,1280]{1,0:T(8,128)(2,1)S(1)}, bf16[128,1280]{1,0:T(8,128)(2,1)S(1)}, u32[]{:S(2)}, u32[]{:S(2)}) collective-permute-start(bf16[128,1280]{1,0:T(8,128)(2,1)S(1)} %copy.13), channel_id=1, source_target_pairs={{0,4},{4,8},{8,12},{12,16},{16,20},{20,24},{24,28},{28,32},{32,36}... | collective-permute-start | bytes 983048 | tf_op jit(solution)/shard_map/while/body/eval_jaxpr/ppermute | solution.py:12
  699.3 45.2 %reduce-scatter.5.cloned.1.call-start = ((), (), s32[]{:S(2)}) async-start(), calls=%async_computation.4 | async-start | bytes 327680 | tf_op jit(solution)/shard_map/while/body/eval_jaxpr/reduce_scatter | solution.py:33
  748.2 45.4 %reduce-scatter.5.cloned.1.call-start = ((), (), s32[]{:S(2)}) async-start(), calls=%async_computation.4 | async-start | bytes 327680 | tf_op jit(solution)/shard_map/while/body/eval_jaxpr/reduce_scatter | solution.py:33
  749.5 45.1 %collective-permute-start = (bf16[128,1280]{1,0:T(8,128)(2,1)S(1)}, bf16[128,1280]{1,0:T(8,128)(2,1)S(1)}, u32[]{:S(2)}, u32[]{:S(2)}) collective-permute-start(bf16[128,1280]{1,0:T(8,128)(2,1)S(1)} %copy.13), channel_id=1, source_target_pairs={{0,4},{4,8},{8,12},{12,16},{16,20},{20,24},{24,28},{28,32},{32,36}... | collective-permute-start | bytes 983048 | tf_op jit(solution)/shard_map/while/body/eval_jaxpr/ppermute | solution.py:12
  797.2 45.4 %reduce-scatter.5.cloned.1.call-start = ((), (), s32[]{:S(2)}) async-start(), calls=%async_computation.4 | async-start | bytes 327680 | tf_op jit(solution)/shard_map/while/body/eval_jaxpr/reduce_scatter | solution.py:33
  798.5 45.2 %collective-permute-start = (bf16[128,1280]{1,0:T(8,128)(2,1)S(1)}, bf16[128,1280]{1,0:T(8,128)(2,1)S(1)}, u32[]{:S(2)}, u32[]{:S(2)}) collective-permute-start(bf16[128,1280]{1,0:T(8,128)(2,1)S(1)} %copy.13), channel_id=1, source_target_pairs={{0,4},{4,8},{8,12},{12,16},{16,20},{20,24},{24,28},{28,32},{32,36}... | collective-permute-start | bytes 983048 | tf_op jit(solution)/shard_map/while/body/eval_jaxpr/ppermute | solution.py:12
  846.3 45.2 %reduce-scatter.5.cloned.1.call-start = ((), (), s32[]{:S(2)}) async-start(), calls=%async_computation.4 | async-start | bytes 327680 | tf_op jit(solution)/shard_map/while/body/eval_jaxpr/reduce_scatter | solution.py:33
  895.2 45.4 %reduce-scatter.5.cloned.1.call-start = ((), (), s32[]{:S(2)}) async-start(), calls=%async_computation.4 | async-start | bytes 327680 | tf_op jit(solution)/shard_map/while/body/eval_jaxpr/reduce_scatter | solution.py:33
  896.5 45.1 %collective-permute-start = (bf16[128,1280]{1,0:T(8,128)(2,1)S(1)}, bf16[128,1280]{1,0:T(8,128)(2,1)S(1)}, u32[]{:S(2)}, u32[]{:S(2)}) collective-permute-start(bf16[128,1280]{1,0:T(8,128)(2,1)S(1)} %copy.13), channel_id=1, source_target_pairs={{0,4},{4,8},{8,12},{12,16},{16,20},{20,24},{24,28},{28,32},{32,36}... | collective-permute-start | bytes 983048 | tf_op jit(solution)/shard_map/while/body/eval_jaxpr/ppermute | solution.py:12
  944.2 45.4 %reduce-scatter.5.cloned.1.call-start = ((), (), s32[]{:S(2)}) async-start(), calls=%async_computation.4 | async-start | bytes 327680 | tf_op jit(solution)/shard_map/while/body/eval_jaxpr/reduce_scatter | solution.py:33
  945.5 45.1 %collective-permute-start = (bf16[128,1280]{1,0:T(8,128)(2,1)S(1)}, bf16[128,1280]{1,0:T(8,128)(2,1)S(1)}, u32[]{:S(2)}, u32[]{:S(2)}) collective-permute-start(bf16[128,1280]{1,0:T(8,128)(2,1)S(1)} %copy.13), channel_id=1, source_target_pairs={{0,4},{4,8},{8,12},{12,16},{16,20},{20,24},{24,28},{28,32},{32,36}... | collective-permute-start | bytes 983048 | tf_op jit(solution)/shard_map/while/body/eval_jaxpr/ppermute | solution.py:12
  993.2 45.3 %reduce-scatter.5.cloned.1.call-start = ((), (), s32[]{:S(2)}) async-start(), calls=%async_computation.4 | async-start | bytes 327680 | tf_op jit(solution)/shard_map/while/body/eval_jaxpr/reduce_scatter | solution.py:33
  994.5 45.1 %collective-permute-start = (bf16[128,1280]{1,0:T(8,128)(2,1)S(1)}, bf16[128,1280]{1,0:T(8,128)(2,1)S(1)}, u32[]{:S(2)}, u32[]{:S(2)}) collective-permute-start(bf16[128,1280]{1,0:T(8,128)(2,1)S(1)} %copy.13), channel_id=1, source_target_pairs={{0,4},{4,8},{8,12},{12,16},{16,20},{20,24},{24,28},{28,32},{32,36}... | collective-permute-start | bytes 983048 | tf_op jit(solution)/shard_map/while/body/eval_jaxpr/ppermute | solution.py:12
  1042.3 45.4 %reduce-scatter.5.cloned.1.call-start = ((), (), s32[]{:S(2)}) async-start(), calls=%async_computation.4 | async-start | bytes 327680 | tf_op jit(solution)/shard_map/while/body/eval_jaxpr/reduce_scatter | solution.py:33
  1043.6 45.1 %collective-permute-start = (bf16[128,1280]{1,0:T(8,128)(2,1)S(1)}, bf16[128,1280]{1,0:T(8,128)(2,1)S(1)}, u32[]{:S(2)}, u32[]{:S(2)}) collective-permute-start(bf16[128,1280]{1,0:T(8,128)(2,1)S(1)} %copy.13), channel_id=1, source_target_pairs={{0,4},{4,8},{8,12},{12,16},{16,20},{20,24},{24,28},{28,32},{32,36}... | collective-permute-start | bytes 983048 | tf_op jit(solution)/shard_map/while/body/eval_jaxpr/ppermute | solution.py:12
  1091.3 45.2 %reduce-scatter.5.cloned.1.call-start = ((), (), s32[]{:S(2)}) async-start(), calls=%async_computation.4 | async-start | bytes 327680 | tf_op jit(solution)/shard_map/while/body/eval_jaxpr/reduce_scatter | solution.py:33
  1140.2 45.2 %reduce-scatter.5.cloned.1.call-start = ((), (), s32[]{:S(2)}) async-start(), calls=%async_computation.4 | async-start | bytes 327680 | tf_op jit(solution)/shard_map/while/body/eval_jaxpr/reduce_scatter | solution.py:33
  1189.1 45.4 %reduce-scatter.5.cloned.1.call-start = ((), (), s32[]{:S(2)}) async-start(), calls=%async_computation.4 | async-start | bytes 327680 | tf_op jit(solution)/shard_map/while/body/eval_jaxpr/reduce_scatter | solution.py:33
  1190.4 45.1 %collective-permute-start = (bf16[128,1280]{1,0:T(8,128)(2,1)S(1)}, bf16[128,1280]{1,0:T(8,128)(2,1)S(1)}, u32[]{:S(2)}, u32[]{:S(2)}) collective-permute-start(bf16[128,1280]{1,0:T(8,128)(2,1)S(1)} %copy.13), channel_id=1, source_target_pairs={{0,4},{4,8},{8,12},{12,16},{16,20},{20,24},{24,28},{28,32},{32,36}... | collective-permute-start | bytes 983048 | tf_op jit(solution)/shard_map/while/body/eval_jaxpr/ppermute | solution.py:12
  1238.1 45.4 %reduce-scatter.5.cloned.1.call-start = ((), (), s32[]{:S(2)}) async-start(), calls=%async_computation.4 | async-start | bytes 327680 | tf_op jit(solution)/shard_map/while/body/eval_jaxpr/reduce_scatter | solution.py:33
  1239.4 45.1 %collective-permute-start = (bf16[128,1280]{1,0:T(8,128)(2,1)S(1)}, bf16[128,1280]{1,0:T(8,128)(2,1)S(1)}, u32[]{:S(2)}, u32[]{:S(2)}) collective-permute-start(bf16[128,1280]{1,0:T(8,128)(2,1)S(1)} %copy.13), channel_id=1, source_target_pairs={{0,4},{4,8},{8,12},{12,16},{16,20},{20,24},{24,28},{28,32},{32,36}... | collective-permute-start | bytes 983048 | tf_op jit(solution)/shard_map/while/body/eval_jaxpr/ppermute | solution.py:12
  1287.2 45.4 %reduce-scatter.5.cloned.1.call-start = ((), (), s32[]{:S(2)}) async-start(), calls=%async_computation.4 | async-start | bytes 327680 | tf_op jit(solution)/shard_map/while/body/eval_jaxpr/reduce_scatter | solution.py:33
  1288.5 45.1 %collective-permute-start = (bf16[128,1280]{1,0:T(8,128)(2,1)S(1)}, bf16[128,1280]{1,0:T(8,128)(2,1)S(1)}, u32[]{:S(2)}, u32[]{:S(2)}) collective-permute-start(bf16[128,1280]{1,0:T(8,128)(2,1)S(1)} %copy.13), channel_id=1, source_target_pairs={{0,4},{4,8},{8,12},{12,16},{16,20},{20,24},{24,28},{28,32},{32,36}... | collective-permute-start | bytes 983048 | tf_op jit(solution)/shard_map/while/body/eval_jaxpr/ppermute | solution.py:12
  1336.2 45.3 %reduce-scatter.5.cloned.1.call-start = ((), (), s32[]{:S(2)}) async-start(), calls=%async_computation.4 | async-start | bytes 327680 | tf_op jit(solution)/shard_map/while/body/eval_jaxpr/reduce_scatter | solution.py:33
  1337.5 45.1 %collective-permute-start = (bf16[128,1280]{1,0:T(8,128)(2,1)S(1)}, bf16[128,1280]{1,0:T(8,128)(2,1)S(1)}, u32[]{:S(2)}, u32[]{:S(2)}) collective-permute-start(bf16[128,1280]{1,0:T(8,128)(2,1)S(1)} %copy.13), channel_id=1, source_target_pairs={{0,4},{4,8},{8,12},{12,16},{16,20},{20,24},{24,28},{28,32},{32,36}... | collective-permute-start | bytes 983048 | tf_op jit(solution)/shard_map/while/body/eval_jaxpr/ppermute | solution.py:12
  1385.3 45.2 %reduce-scatter.5.cloned.1.call-start = ((), (), s32[]{:S(2)}) async-start(), calls=%async_computation.4 | async-start | bytes 327680 | tf_op jit(solution)/shard_map/while/body/eval_jaxpr/reduce_scatter | solution.py:33
  1434.1 45.4 %reduce-scatter.5.cloned.1.call-start = ((), (), s32[]{:S(2)}) async-start(), calls=%async_computation.4 | async-start | bytes 327680 | tf_op jit(solution)/shard_map/while/body/eval_jaxpr/reduce_scatter | solution.py:33
  1435.5 45.1 %collective-permute-start = (bf16[128,1280]{1,0:T(8,128)(2,1)S(1)}, bf16[128,1280]{1,0:T(8,128)(2,1)S(1)}, u32[]{:S(2)}, u32[]{:S(2)}) collective-permute-start(bf16[128,1280]{1,0:T(8,128)(2,1)S(1)} %copy.13), channel_id=1, source_target_pairs={{0,4},{4,8},{8,12},{12,16},{16,20},{20,24},{24,28},{28,32},{32,36}... | collective-permute-start | bytes 983048 | tf_op jit(solution)/shard_map/while/body/eval_jaxpr/ppermute | solution.py:12
  1483.2 45.3 %reduce-scatter.5.cloned.1.call-start = ((), (), s32[]{:S(2)}) async-start(), calls=%async_computation.4 | async-start | bytes 327680 | tf_op jit(solution)/shard_map/while/body/eval_jaxpr/reduce_scatter | solution.py:33
  1484.5 45.1 %collective-permute-start = (bf16[128,1280]{1,0:T(8,128)(2,1)S(1)}, bf16[128,1280]{1,0:T(8,128)(2,1)S(1)}, u32[]{:S(2)}, u32[]{:S(2)}) collective-permute-start(bf16[128,1280]{1,0:T(8,128)(2,1)S(1)} %copy.13), channel_id=1, source_target_pairs={{0,4},{4,8},{8,12},{12,16},{16,20},{20,24},{24,28},{28,32},{32,36}... | collective-permute-start | bytes 983048 | tf_op jit(solution)/shard_map/while/body/eval_jaxpr/ppermute | solution.py:12
  (80 other events, 3057.6 us)
Sparse Core Ops, SparseCore 0:
  12.6 32.2 reduce-scatter.2
  63.8 29.7 reduce-scatter.2
  112.3 30.0 reduce-scatter.2
  161.6 29.7 reduce-scatter.2
  193.8 12.4 reduce-scatter.4
  210.6 29.7 reduce-scatter.2
  259.5 29.7 reduce-scatter.2
  308.4 29.7 reduce-scatter.2
  357.0 30.0 reduce-scatter.2
  405.9 30.0 reduce-scatter.2
  455.1 29.7 reduce-scatter.2
  487.2 12.4 reduce-scatter.4
  504.0 29.7 reduce-scatter.2
  553.0 29.7 reduce-scatter.2
  585.2 12.4 reduce-scatter.4
  601.9 29.7 reduce-scatter.2
  650.5 30.0 reduce-scatter.2
  699.9 29.7 reduce-scatter.2
  748.7 29.7 reduce-scatter.2
  781.0 12.4 reduce-scatter.4
  797.5 30.0 reduce-scatter.2
  830.1 12.4 reduce-scatter.4
  846.9 29.7 reduce-scatter.2
  895.4 30.0 reduce-scatter.2
  928.0 12.4 reduce-scatter.4
  944.5 29.7 reduce-scatter.2
  976.8 12.7 reduce-scatter.4
  993.8 29.7 reduce-scatter.2
  1042.6 30.0 reduce-scatter.2
  1075.1 12.4 reduce-scatter.4
  1091.6 30.0 reduce-scatter.2
  1124.0 12.4 reduce-scatter.4
  1140.5 29.7 reduce-scatter.2
  1172.6 12.7 reduce-scatter.4
  1189.4 29.7 reduce-scatter.2
  1221.6 12.7 reduce-scatter.4
  1238.4 29.7 reduce-scatter.2
  1270.7 12.7 reduce-scatter.4
  1287.5 29.7 reduce-scatter.2
  1319.7 12.7 reduce-scatter.4
  1336.8 29.4 reduce-scatter.2
  1368.8 12.7 reduce-scatter.4
  1385.8 29.4 reduce-scatter.2
  1417.7 12.7 reduce-scatter.4
  1434.4 29.7 reduce-scatter.2
  1466.7 12.7 reduce-scatter.4
  1483.8 29.4 reduce-scatter.2
  1515.8 12.7 reduce-scatter.4
  (14 shorter events, 173.2 us)
Sparse Core Ops, SparseCore 1:
  1532.6 38.5 all-reduce.4
where the time goes:
time: 1590 us
  waiting for transfers between devices  1330 us (84%)
  matrix products  116 us (7%)
  starting transfers between devices  78.5 us (5%)
  other arithmetic  34.8 us (2%)
    reduce_scatter x31, waiting for transfers between devices, pair_terms(): lax.psum_scatter(part_act, 'tensor', scatter_dimension=1, tiled=True)  825 us
    reduce_scatter x31, waiting for transfers between devices, pair_terms(): lax.psum_scatter(part_grad, 'tensor', scatter_dimension=1, tiled=True)  465 us
    dot_general x32, matrix products, pair_terms(): jnp.einsum('ntd,sd->nts', train_act, block_act, preferred_element_type=jn...  78.4 us
    ppermute x62, starting transfers between devices, passed_along(): return lax.ppermute(value, axis, pairs)  76.1 us
    dot_general x32, matrix products, pair_terms(): jnp.einsum('ntd,sd->nts', train_grad, block_grad, preferred_element_type=...  37.7 us
    unnamed x2, waiting for transfers between devices  37.4 us
  transfers between devices with their start and end apart: 125, of which 63 were waited for; matrix products, arithmetic and copies ran while one was open for 5% of the time, Pallas kernels for 0%

commit v1 on v0

v1 whole, which is shorter than its diff:
```python
import functools

import jax
import jax.numpy as jnp
from jax import lax
from jax.experimental import pallas as pl
from jax.experimental.pallas import tpu as pltpu
from jax.sharding import PartitionSpec as P

MESH = pl.DeviceIdType.MESH
RING = 4


def kernel(
    total_width,
    train_act,
    train_grad,
    val_act,
    val_grad,
    out_ref,
    trains,
    vals,
    grams,
    from_core,
    sums,
    tiles,
    arrived,
    local_sem,
    send_sem,
    recv_sem,
):
    seq_len = train_act.shape[1]
    train_in = (train_act, train_grad)
    val_in = (val_act, val_grad)

    dp = lax.axis_index("dp")
    tensor = lax.axis_index("tensor")
    z_hi, y, x = dp // 16, (dp // 4) % 4, dp % 4
    z_lo, core = tensor // 2, tensor % 2

    def at(z_hi, y, x, z_lo, core):
        return (z_hi * 16 + y * 4 + x, z_lo * 2 + core)

    x_next, x_prev = (x + 1) % 4, (x + 3) % 4
    y_next, y_prev = (y + 1) % 4, (y + 3) % 4
    to_x_next = at(z_hi, y, x_next, z_lo, core)
    to_x_prev = at(z_hi, y, x_prev, z_lo, core)
    to_y_next = at(z_hi, y_next, x, z_lo, core)
    to_y_prev = at(z_hi, y_prev, x, z_lo, core)
    to_lo = at(z_hi, y, x, 1 - z_lo, core)
    to_hi = at(1 - z_hi, y, x, 1 - z_lo, core)
    to_core = at(z_hi, y, x, z_lo, 1 - core)
    x_at = (x, x_prev, x_next, (x + 2) % 4)
    y_at = (y, y_prev, y_next, (y + 2) % 4)

    mine = pl.ds(z_lo * 2, 2)
    theirs = pl.ds((1 - z_lo) * 2, 2)
    local = []
    for m in range(2):
        local.append(
            pltpu.make_async_copy(train_in[m].at[mine], trains.at[m, 0, 0], local_sem.at[m])
        )
        local.append(
            pltpu.make_async_copy(val_in[m], vals.at[m, 0, 0, pl.ds(0, 1)], local_sem.at[2 + m])
        )
    for copy in local:
        copy.start()

    group = [
        (b, d, at(z_hi, y, x_at[b], *((z_lo, core), (z_lo, 1 - core), (1 - z_lo, core), (1 - z_lo, 1 - core))[d]))
        for b in range(RING)
        for d in range(4)
        if (b, d) != (0, 0)
    ]
    barrier = pltpu.get_barrier_semaphore()
    partners = [device for _, _, device in group] + [to_y_next, to_y_prev, to_hi]
    for device in partners:
        pl.semaphore_signal(barrier, inc=1, device_id=device, device_id_type=MESH)
    pl.semaphore_wait(barrier, len(partners))

    copies = {}

    def send(name, src, dst, device):
        key = len(copies)
        copies[name] = pltpu.make_async_remote_copy(
            src_ref=src,
            dst_ref=dst,
            send_sem=send_sem.at[key],
            recv_sem=recv_sem.at[key],
            device_id=device,
            device_id_type=MESH,
        )
        copies[name].start()

    def got(name):
        copies[name].wait_recv()

    def x_direct(s, m):
        src = train_in[m].at[mine] if s == 0 else trains.at[m, 1, 0]
        send(("x", s, m, 1), src, trains.at[m, s, 1], to_x_next)
        send(("x", s, m, 2), src, trains.at[m, s, 2], to_x_prev)

    def x_forward(s, m):
        got(("x", s, m, 1 + m))
        send(("x", s, m, 3), trains.at[m, s, 1 + m], trains.at[m, s, 3], (to_x_next, to_x_prev)[m])

    def x_near(s, m):
        got(("x", s, m, 2 - m))

    def x_far(s, m):
        got(("x", s, m, 3))

    def y_direct(s, w, m):
        src = val_in[m] if (s, w) == (0, 0) else vals.at[m, s, 0, pl.ds(w, 1)]
        send(("y", s, w, m, 1), src, vals.at[m, s, 1, pl.ds(w, 1)], to_y_next)
        send(("y", s, w, m, 2), src, vals.at[m, s, 2, pl.ds(w, 1)], to_y_prev)

    def y_forward(s, w, m):
        got(("y", s, w, m, 1 + m))
        here = vals.at[m, s, 1 + m, pl.ds(w, 1)]
        send(("y", s, w, m, 3), here, vals.at[m, s, 3, pl.ds(w, 1)], (to_y_next, to_y_prev)[m])

    def y_rest(s, w, m):
        got(("y", s, w, m, 2 - m))
        got(("y", s, w, m, 3))

    def gram(s, blocks):
        def one(i, carry):
            v, m = i // 2, i % 2
            for b in blocks:
                left = trains[m, s, b].reshape(2 * seq_len, -1)
                right = vals[m, s, v].reshape(2 * seq_len, -1)
                part = lax.dot_general(
                    left, right, (((1,), (1,)), ((), ())), preferred_element_type=jnp.float32
                )
                for r in range(2):
                    rows = part[r * seq_len : (r + 1) * seq_len]
                    if s == 0:
                        grams[b, v, r, m] = rows
                    else:
                        grams[b, v, r, m] += rows
            return carry

        lax.fori_loop(0, 2 * RING, one, 0)

    for m in range(2):
        send(("lo", m), val_in[m], vals.at[m, 1, 0, pl.ds(0, 1)], to_lo)
        send(("hi", m), val_in[m], vals.at[m, 1, 0, pl.ds(1, 1)], to_hi)
        y_direct(0, 0, m)
        x_direct(0, m)
    for m in range(2):
        send(("swap", m), train_in[m].at[theirs], trains.at[m, 1, 0], to_lo)

    def hand_over(m):
        got(("lo", m))
        send(("far", m), vals.at[m, 1, 0, pl.ds(0, 1)], vals.at[m, 0, 0, pl.ds(1, 1)], to_hi)
        y_direct(1, 0, m)

    def take_hi(m):
        got(("hi", m))
        y_direct(1, 1, m)

    def take_far(m):
        got(("far", m))
        y_direct(0, 1, m)

    def take_swap(m):
        got(("swap", m))
        x_direct(1, m)

    for m in range(2):
        y_forward(0, 0, m)
        hand_over(m)
        take_hi(m)
    x_forward(0, 0)
    x_forward(0, 1)
    take_far(0)
    take_far(1)
    take_swap(0)
    take_swap(1)
    for copy in local:
        copy.wait()
    for m in range(2):
        y_rest(0, 0, m)
    for w, s in ((1, 1), (0, 1), (1, 0)):
        for m in range(2):
            y_forward(s, w, m)
    for m in range(2):
        x_near(0, m)
        x_far(0, m)
        y_rest(0, 1, m)
    x_forward(1, 0)
    gram(0, (0, 1))
    x_forward(1, 1)
    gram(0, (2, 3))
    for m in range(2):
        y_rest(1, 0, m)
        y_rest(1, 1, m)
        x_near(1, m)
    gram(1, (0, 1))
    for m in range(2):
        x_far(1, m)
    gram(1, (2, 3))

    for b in range(RING):
        for v in range(RING):
            send(("core", b, v), grams.at[b, v, 1 - core], from_core.at[b, v], to_core)
    lane = lax.broadcasted_iota(jnp.int32, (8, 128), 1)
    row = lax.broadcasted_iota(jnp.int32, (8, 128), 0)
    sums[...] = jnp.zeros_like(sums)
    for b in range(RING):
        for v in range(RING):
            got(("core", b, v))
            act = grams[b, v, core, 0] + from_core[b, v, 0]
            grad = grams[b, v, core, 1] + from_core[b, v, 1]
            sums[pl.ds(b, 1), pl.ds(v * 2 * seq_len, 2 * seq_len)] = jnp.sum(
                act * grad, axis=0, keepdims=True
            )
    scores = jnp.zeros((8, 128), jnp.float32)
    for v in range(RING):
        for w in range(2):
            first = (v * 2 + w) * seq_len
            one = jnp.sum(sums[:, first : first + seq_len], axis=1, keepdims=True)
            column = (z_hi if w == 0 else 1 - z_hi) * 16 + y_at[v] * 4 + x
            scores = jnp.where(lane == column, one, scores)
    scores = scores * (1.0 / (total_width * seq_len))
    for b in range(RING):
        tiles[b] = jnp.where(row == 2 * z_lo + core, jnp.broadcast_to(scores[b : b + 1], (8, 128)), 0.0)
    for b, d, device in group:
        send(("out", b, d), tiles.at[b], arrived.at[b, d], device)
    total = tiles[0]
    for b, d, _ in group:
        got(("out", b, d))
        total = total + arrived[b, d]
    out_ref[...] = total[: out_ref.shape[0], : out_ref.shape[1]]
    for copy in copies.values():
        copy.wait_send()


N_COPIES = 12 + 24 + 6 + 2 + 16 + 15


def per_device(train_act, train_grad, val_act, val_grad):
    n_train, seq_len, width = train_act.shape
    n_val = lax.axis_size("dp")
    bf16, f32 = train_act.dtype, jnp.float32
    anywhere = pl.BlockSpec(memory_space=pl.ANY)
    return pl.pallas_call(
        functools.partial(kernel, width * lax.axis_size("tensor")),
        out_shape=jax.ShapeDtypeStruct((n_train, n_val), f32),
        in_specs=[anywhere] * 4,
        out_specs=pl.BlockSpec(memory_space=pltpu.VMEM),
        scratch_shapes=[
            pltpu.VMEM((2, 2, RING, 2, seq_len, width), bf16),
            pltpu.VMEM((2, 2, RING, 2, seq_len, width), bf16),
            pltpu.VMEM((RING, RING, 2, 2, seq_len, 2 * seq_len), f32),
            pltpu.VMEM((RING, RING, 2, seq_len, 2 * seq_len), f32),
            pltpu.VMEM((8, RING * 2 * seq_len), f32),
            pltpu.VMEM((RING, 8, 128), f32),
            pltpu.VMEM((RING, 4, 8, 128), f32),
            pltpu.SemaphoreType.DMA((4,)),
            pltpu.SemaphoreType.DMA((N_COPIES,)),
            pltpu.SemaphoreType.DMA((N_COPIES,)),
        ],
        compiler_params=pltpu.CompilerParams(
            collective_id=0, has_side_effects=True, vmem_limit_bytes=56 * 1024 * 1024
        ),
        cost_estimate=pl.CostEstimate(
            flops=4 * 64 * (2 * seq_len) ** 2 * width, bytes_accessed=3_300_000, transcendentals=0
        ),
    )(train_act, train_grad, val_act, val_grad)


def solution(mesh):
    placed = P("dp", None, "tensor")
    return jax.shard_map(
        per_device, mesh=mesh, in_specs=(placed,) * 4, out_specs=P("dp", None), check_vma=False
    )
```

time: 1590 us -> 132 us (0.08)
  waiting for transfers between devices: 1330 us -> 0 us
  Pallas kernels: 0 us -> 131 us
  matrix products: 116 us -> 0 us
  starting transfers between devices: 78.5 us -> 0 us
  other arithmetic: 34.8 us -> 0 us
    reduce_scatter x62 -> x0, waiting for transfers between devices: 1290 us -> none  [the longest x31 825 us: pair_terms(): lax.psum_scatter(part_act, 'tensor', scatter_dimension=1, tiled=True)]
    pallas_call x0 -> x1, Pallas kernels: none -> 131 us  [per_device(): pl.pallas_call(functools.partial(kernel, width * lax.axis_size('tensor'))...]
    dot_general x64 -> x0, matrix products: 116 us -> none  [the longest x32 78.4 us: pair_terms(): jnp.einsum('ntd,sd->nts', train_act, block_act, preferred_element_type=jn...]
    ppermute x62 -> x0, starting transfers between devices: 76.1 us -> none  [passed_along(): return lax.ppermute(value, axis, pairs)]
    unnamed x2 -> x0, waiting for transfers between devices: 37.4 us -> none
    reduce_sum x32 -> x0, other arithmetic: 31.6 us -> none  [accumulate(): return place(scores, column, jnp.sum(terms, axis=1))]
  transfers between devices with their start and end apart: 125 -> 0, of which waited for: 63 -> 0; matrix products, arithmetic and copies ran while one was open for 5% -> 0% of each run, Pallas kernels for 0% -> 0%
where the time goes in v1:
time: 132 us
  Pallas kernels  131 us (99%)
    pallas_call x1, Pallas kernels, per_device(): pl.pallas_call(functools.partial(kernel, width * lax.axis_size('tensor'))...  131 us

profile of v1, /device:TPU:1, one launch (start us, length us, event | category | flops | bytes accessed | tf_op | source)
XLA Modules:
  0.0 132.1 jit_solution(9209411844313794605)
XLA Ops:
  0.0 130.8 %shard_map.46 = f32[4,32]{1,0:T(4,128)} custom-call(bf16[4,128,1280]{2,1,0:T(8,128)(2,1)} %train_act.1, bf16[4,128,1280]{2,1,0:T(8,128)(2,1)} %train_grad.1, bf16[1,128,1280]{2,1,0:T(8,128)(2,1)} %val_act.1, bf16[1,128,1280]{2,1,0:T(8,128)(2,1)} %val_grad.1), custom_call_target="tpu_custom_call" | custom-call | flops 21474836480 | bytes 3300000 | tf_op jit(solution)/shard_map/pallas_call | solution.py:248
  130.8 1.3 copy.6

commit v2 on v1

--- a/solution.py
+++ b/solution.py
@@ -28,6 +28,8 @@
     local_sem,
     send_sem,
     recv_sem,
+    core_send_sem,
+    core_recv_sem,
 ):
     seq_len = train_act.shape[1]
     train_in = (train_act, train_grad)
@@ -73,7 +75,7 @@
         if (b, d) != (0, 0)
     ]
     barrier = pltpu.get_barrier_semaphore()
-    partners = [device for _, _, device in group] + [to_y_next, to_y_prev, to_hi]
+    partners = [to_x_next, to_x_prev, to_y_next, to_y_prev, to_lo, to_hi, to_core]
     for device in partners:
         pl.semaphore_signal(barrier, inc=1, device_id=device, device_id_type=MESH)
     pl.semaphore_wait(barrier, len(partners))
@@ -97,37 +99,54 @@
 
     def x_direct(s, m):
         src = train_in[m].at[mine] if s == 0 else trains.at[m, 1, 0]
-        send(("x", s, m, 1), src, trains.at[m, s, 1], to_x_next)
-        send(("x", s, m, 2), src, trains.at[m, s, 2], to_x_prev)
+        ways = [(1, to_x_next), (2, to_x_prev)]
+        for place, device in ways if m == 0 else ways[::-1]:
+            send(("x", s, m, place), src, trains.at[m, s, place], device)
 
     def x_forward(s, m):
         got(("x", s, m, 1 + m))
         send(("x", s, m, 3), trains.at[m, s, 1 + m], trains.at[m, s, 3], (to_x_next, to_x_prev)[m])
 
-    def x_near(s, m):
-        got(("x", s, m, 2 - m))
-
-    def x_far(s, m):
-        got(("x", s, m, 3))
+    def x_near(s):
+        for m in range(2):
+            got(("x", s, m, 2 - m))
+
+    def x_far(s):
+        for m in range(2):
+            got(("x", s, m, 3))
 
     def y_direct(s, w, m):
         src = val_in[m] if (s, w) == (0, 0) else vals.at[m, s, 0, pl.ds(w, 1)]
-        send(("y", s, w, m, 1), src, vals.at[m, s, 1, pl.ds(w, 1)], to_y_next)
-        send(("y", s, w, m, 2), src, vals.at[m, s, 2, pl.ds(w, 1)], to_y_prev)
+        ways = [(1, to_y_next), (2, to_y_prev)]
+        for place, device in ways if m == 0 else ways[::-1]:
+            send(("y", s, w, m, place), src, vals.at[m, s, place, pl.ds(w, 1)], device)
 
     def y_forward(s, w, m):
         got(("y", s, w, m, 1 + m))
         here = vals.at[m, s, 1 + m, pl.ds(w, 1)]
         send(("y", s, w, m, 3), here, vals.at[m, s, 3, pl.ds(w, 1)], (to_y_next, to_y_prev)[m])
 
-    def y_rest(s, w, m):
-        got(("y", s, w, m, 2 - m))
-        got(("y", s, w, m, 3))
-
-    def gram(s, blocks):
-        def one(i, carry):
-            v, m = i // 2, i % 2
-            for b in blocks:
+    def y_near(s, w):
+        for m in range(2):
+            got(("y", s, w, m, 2 - m))
+
+    def y_far(s, w):
+        for m in range(2):
+            got(("y", s, w, m, 3))
+
+    def core_copy(b, v):
+        return pltpu.make_async_remote_copy(
+            src_ref=grams.at[b, v, 1 - core],
+            dst_ref=from_core.at[b, v],
+            send_sem=core_send_sem.at[b, v],
+            recv_sem=core_recv_sem.at[b, v],
+            device_id=to_core,
+            device_id_type=MESH,
+        )
+
+    def gram(s, b, first, last):
+        def one(v, carry):
+            for m in range(2):
                 left = trains[m, s, b].reshape(2 * seq_len, -1)
                 right = vals[m, s, v].reshape(2 * seq_len, -1)
                 part = lax.dot_general(
@@ -139,88 +158,94 @@
                         grams[b, v, r, m] = rows
                     else:
                         grams[b, v, r, m] += rows
+            if s == 1:
+                core_copy(b, v).start()
             return carry
 
-        lax.fori_loop(0, 2 * RING, one, 0)
-
+        lax.fori_loop(first, last, one, 0)
+
+    def finish(b, first, last):
+        def one(v, carry):
+            core_copy(b, v).wait_recv()
+            act = grams[b, v, core, 0] + from_core[b, v, 0]
+            grad = grams[b, v, core, 1] + from_core[b, v, 1]
+            sums[v, pl.ds(b, 1)] = jnp.sum(act * grad, axis=0, keepdims=True)
+            return carry
+
+        lax.fori_loop(first, last, one, 0)
+
+    sums[...] = jnp.zeros_like(sums)
+    for m in range(2):
+        x_direct(0, m)
+        y_direct(0, 0, m)
+        send(("hi", m), val_in[m], vals.at[m, 1, 0, pl.ds(1, 1)], to_hi)
+    send(("swap", 0), train_in[0].at[theirs], trains.at[0, 1, 0], to_lo)
     for m in range(2):
         send(("lo", m), val_in[m], vals.at[m, 1, 0, pl.ds(0, 1)], to_lo)
-        send(("hi", m), val_in[m], vals.at[m, 1, 0, pl.ds(1, 1)], to_hi)
-        y_direct(0, 0, m)
-        x_direct(0, m)
-    for m in range(2):
-        send(("swap", m), train_in[m].at[theirs], trains.at[m, 1, 0], to_lo)
-
-    def hand_over(m):
+    for copy in local:
+        copy.wait()
+
+    for m in range(2):
+        y_forward(0, 0, m)
+    for m in range(2):
+        got(("hi", m))
+        y_direct(1, 1, m)
+    x_forward(0, 0)
+    x_forward(0, 1)
+    got(("swap", 0))
+    x_direct(1, 0)
+    for m in range(2):
         got(("lo", m))
         send(("far", m), vals.at[m, 1, 0, pl.ds(0, 1)], vals.at[m, 0, 0, pl.ds(1, 1)], to_hi)
-        y_direct(1, 0, m)
-
-    def take_hi(m):
-        got(("hi", m))
-        y_direct(1, 1, m)
-
-    def take_far(m):
+    send(("swap", 1), train_in[1].at[theirs], trains.at[1, 1, 0], to_lo)
+    y_near(0, 0)
+    y_far(0, 0)
+    for m in range(2):
+        y_forward(1, 1, m)
+    for m in range(2):
         got(("far", m))
         y_direct(0, 1, m)
-
-    def take_swap(m):
-        got(("swap", m))
-        x_direct(1, m)
-
-    for m in range(2):
-        y_forward(0, 0, m)
-        hand_over(m)
-        take_hi(m)
-    x_forward(0, 0)
-    x_forward(0, 1)
-    take_far(0)
-    take_far(1)
-    take_swap(0)
-    take_swap(1)
-    for copy in local:
-        copy.wait()
-    for m in range(2):
-        y_rest(0, 0, m)
-    for w, s in ((1, 1), (0, 1), (1, 0)):
-        for m in range(2):
-            y_forward(s, w, m)
-    for m in range(2):
-        x_near(0, m)
-        x_far(0, m)
-        y_rest(0, 1, m)
+    got(("swap", 1))
+    x_direct(1, 1)
+    x_near(0)
+    x_far(0)
+    y_near(1, 1)
+    y_far(1, 1)
+    for m in range(2):
+        y_direct(1, 0, m)
+    for m in range(2):
+        y_forward(0, 1, m)
     x_forward(1, 0)
-    gram(0, (0, 1))
+    y_near(0, 1)
+    y_far(0, 1)
+    gram(0, 0, 0, RING)
+    gram(0, 1, 0, RING)
     x_forward(1, 1)
-    gram(0, (2, 3))
-    for m in range(2):
-        y_rest(1, 0, m)
-        y_rest(1, 1, m)
-        x_near(1, m)
-    gram(1, (0, 1))
-    for m in range(2):
-        x_far(1, m)
-    gram(1, (2, 3))
-
-    for b in range(RING):
-        for v in range(RING):
-            send(("core", b, v), grams.at[b, v, 1 - core], from_core.at[b, v], to_core)
+    for m in range(2):
+        y_forward(1, 0, m)
+    gram(0, 2, 0, RING)
+    gram(0, 3, 0, RING)
+    x_near(1)
+    y_near(1, 0)
+    for b in range(3):
+        gram(1, b, 0, 3)
+    for b in range(3):
+        finish(b, 0, 3)
+    y_far(1, 0)
+    for b in range(3):
+        gram(1, b, 3, RING)
+    x_far(1)
+    gram(1, 3, 0, RING)
+    for b in range(3):
+        finish(b, 3, RING)
+    finish(3, 0, RING)
+
     lane = lax.broadcasted_iota(jnp.int32, (8, 128), 1)
     row = lax.broadcasted_iota(jnp.int32, (8, 128), 0)
-    sums[...] = jnp.zeros_like(sums)
-    for b in range(RING):
-        for v in range(RING):
-            got(("core", b, v))
-            act = grams[b, v, core, 0] + from_core[b, v, 0]
-            grad = grams[b, v, core, 1] + from_core[b, v, 1]
-            sums[pl.ds(b, 1), pl.ds(v * 2 * seq_len, 2 * seq_len)] = jnp.sum(
-                act * grad, axis=0, keepdims=True
-            )
     scores = jnp.zeros((8, 128), jnp.float32)
     for v in range(RING):
         for w in range(2):
-            first = (v * 2 + w) * seq_len
-            one = jnp.sum(sums[:, first : first + seq_len], axis=1, keepdims=True)
+            one = jnp.sum(sums[v, :, w * seq_len : (w + 1) * seq_len], axis=1, keepdims=True)
             column = (z_hi if w == 0 else 1 - z_hi) * 16 + y_at[v] * 4 + x
             scores = jnp.where(lane == column, one, scores)
     scores = scores * (1.0 / (total_width * seq_len))
@@ -235,9 +260,12 @@
     out_ref[...] = total[: out_ref.shape[0], : out_ref.shape[1]]
     for copy in copies.values():
         copy.wait_send()
-
-
-N_COPIES = 12 + 24 + 6 + 2 + 16 + 15
+    for b in range(RING):
+        for v in range(RING):
+            core_copy(b, v).wait_send()
+
+
+N_COPIES = 12 + 24 + 6 + 2 + 15
 
 
 def per_device(train_act, train_grad, val_act, val_grad):
@@ -255,12 +283,14 @@
             pltpu.VMEM((2, 2, RING, 2, seq_len, width), bf16),
             pltpu.VMEM((RING, RING, 2, 2, seq_len, 2 * seq_len), f32),
             pltpu.VMEM((RING, RING, 2, seq_len, 2 * seq_len), f32),
-            pltpu.VMEM((8, RING * 2 * seq_len), f32),
+            pltpu.VMEM((RING, 8, 2 * seq_len), f32),
             pltpu.VMEM((RING, 8, 128), f32),
             pltpu.VMEM((RING, 4, 8, 128), f32),
             pltpu.SemaphoreType.DMA((4,)),
             pltpu.SemaphoreType.DMA((N_COPIES,)),
             pltpu.SemaphoreType.DMA((N_COPIES,)),
+            pltpu.SemaphoreType.DMA((RING, RING)),
+            pltpu.SemaphoreType.DMA((RING, RING)),
         ],
         compiler_params=pltpu.CompilerParams(
             collective_id=0, has_side_effects=True, vmem_limit_bytes=56 * 1024 * 1024

time: 132 us -> 117 us (0.89)
  Pallas kernels: 131 us -> 115 us
    pallas_call x1, Pallas kernels: 131 us -> 115 us  [per_device(): pl.pallas_call(functools.partial(kernel, width * lax.axis_size('tensor'))...]
where the time goes in v2:
time: 117 us; the launch traced here: 116 us
  Pallas kernels  115 us (98%)
  local copies, waits for them, and re-layouts  1.26 us (1%)
    pallas_call x1, Pallas kernels, per_device(): pl.pallas_call(functools.partial(kernel, width * lax.axis_size('tensor'))...  115 us

profile of v2, /device:TPU:1, one launch (start us, length us, event | category | flops | bytes accessed | tf_op | source)
XLA Modules:
  0.0 116.4 jit_solution(4620987572416870549)
XLA Ops:
  0.0 115.1 %shard_map.46 = f32[4,32]{1,0:T(4,128)} custom-call(bf16[4,128,1280]{2,1,0:T(8,128)(2,1)} %train_act.1, bf16[4,128,1280]{2,1,0:T(8,128)(2,1)} %train_grad.1, bf16[1,128,1280]{2,1,0:T(8,128)(2,1)} %val_act.1, bf16[1,128,1280]{2,1,0:T(8,128)(2,1)} %val_grad.1), custom_call_target="tpu_custom_call" | custom-call | flops 21474836480 | bytes 3300000 | tf_op jit(solution)/shard_map/pallas_call | solution.py:276
  115.1 1.3 %copy.6 = f32[4,32]{1,0:T(4,128)} copy(f32[4,32]{1,0:T(4,128)} %shard_map.46) | data formatting | bytes 1024

commit v3 on v2

v3 whole, which is shorter than its diff:
```python
import functools

import jax
import jax.numpy as jnp
from jax import lax
from jax.experimental import pallas as pl
from jax.experimental.pallas import tpu as pltpu
from jax.sharding import PartitionSpec as P

MESH = pl.DeviceIdType.MESH
RING = 4

PLACES = {"n": (0, 1, 2), "f": (3,)}
VALS = {"o": (0,), "n": (1, 2), "f": (3,)}

ORDER = (
    ("hi", 0), ("lo", 0), ("y", 0, 0, 0, 1), ("y", 0, 0, 0, 2), ("hi", 1), ("lo", 1), ("x", 0, 0, 1),
    ("x", 0, 0, 2), ("y", 0, 0, 1, 1), ("y", 0, 0, 1, 2), ("far", 0), ("y", 1, 1, 0, 1), ("y", 1, 1, 0, 2),
    ("gram", 0, 0, "n", "o"), ("far", 1), ("swap", 0), ("x", 0, 1, 1), ("x", 0, 1, 2), ("y", 1, 0, 0, 1),
    ("y", 1, 0, 0, 2), ("gram", 0, 1, "n", "o"), ("y", 0, 0, 0, 3, 1), ("y", 0, 0, 0, 3, 2),
    ("x", 0, 0, 3, 1), ("x", 0, 0, 3, 2), ("gram", 0, 0, "f", "o"), ("y", 1, 1, 1, 1), ("y", 1, 1, 1, 2),
    ("swap", 1), ("y", 1, 0, 1, 1), ("y", 1, 0, 1, 2), ("y", 0, 0, 1, 3, 1), ("y", 0, 0, 1, 3, 2),
    ("x", 1, 0, 1), ("x", 1, 0, 2), ("gram", 1, 0, "n", "o"), ("zs", 1, 1), ("y", 0, 1, 0, 1),
    ("y", 0, 1, 0, 2), ("x", 0, 1, 3, 1), ("x", 0, 1, 3, 2), ("gram", 0, 0, "n", "n"),
    ("gram", 0, 0, "f", "n"), ("gram", 1, 0, "n", "n"), ("y", 1, 1, 0, 3, 1), ("y", 1, 1, 0, 3, 2),
    ("gram", 0, 1, "f", "o"), ("zs", 1, 2), ("gram", 0, 1, "n", "n"), ("y", 1, 0, 0, 3, 1),
    ("y", 1, 0, 0, 3, 2), ("gram", 0, 1, "f", "n"), ("y", 1, 1, 1, 3, 1), ("y", 1, 1, 1, 3, 2),
    ("y", 1, 0, 1, 3, 1), ("y", 1, 0, 1, 3, 2), ("x", 1, 1, 1), ("x", 1, 1, 2), ("gram", 1, 1, "n", "o"),
    ("gram", 1, 1, "n", "n"), ("y", 0, 1, 0, 3, 1), ("y", 0, 1, 0, 3, 2), ("gram", 0, 0, "n", "f"),
    ("gram", 0, 0, "f", "f"), ("gram", 1, 0, "n", "f"), ("x", 1, 0, 3, 1), ("x", 1, 0, 3, 2),
    ("gram", 1, 0, "f", "o"), ("gram", 1, 0, "f", "n"), ("gram", 1, 0, "f", "f"), ("zs", 1, 3),
    ("gram", 0, 1, "n", "f"), ("gram", 0, 1, "f", "f"), ("gram", 1, 1, "n", "f"), ("out", "n"),
    ("x", 1, 1, 3, 1), ("x", 1, 1, 3, 2), ("gram", 1, 1, "f", "o"), ("gram", 1, 1, "f", "n"),
    ("gram", 1, 1, "f", "f"), ("out", "f"),
)


def kernel(
    total_width,
    train_act,
    train_grad,
    val_act,
    val_grad,
    out_ref,
    trains,
    vals,
    grams,
    from_core,
    sums,
    tiles,
    arrived,
    local_sem,
    send_sem,
    recv_sem,
    core_send_sem,
    core_recv_sem,
):
    seq_len = train_act.shape[1]
    train_in = (train_act, train_grad)
    val_in = (val_act, val_grad)

    dp = lax.axis_index("dp")
    tensor = lax.axis_index("tensor")
    z_hi, y, x = dp // 16, (dp // 4) % 4, dp % 4
    z_lo, core = tensor // 2, tensor % 2

    def at(z_hi, y, x, z_lo, core):
        return (z_hi * 16 + y * 4 + x, z_lo * 2 + core)

    x_at = (x, (x + 3) % 4, (x + 1) % 4, (x + 2) % 4)
    y_at = (y, (y + 3) % 4, (y + 1) % 4, (y + 2) % 4)
    to_x = {1: at(z_hi, y, x_at[2], z_lo, core), 2: at(z_hi, y, x_at[1], z_lo, core)}
    to_y = {1: at(z_hi, y_at[2], x, z_lo, core), 2: at(z_hi, y_at[1], x, z_lo, core)}
    to_lo = at(z_hi, y, x, 1 - z_lo, core)
    to_hi = at(1 - z_hi, y, x, 1 - z_lo, core)
    to_core = at(z_hi, y, x, z_lo, 1 - core)

    mine = pl.ds(z_lo * 2, 2)
    theirs = pl.ds((1 - z_lo) * 2, 2)
    local = []
    for m in range(2):
        local.append(
            pltpu.make_async_copy(train_in[m].at[mine], trains.at[m, 0, 0], local_sem.at[m])
        )
        local.append(
            pltpu.make_async_copy(val_in[m], vals.at[m, 0, 0, pl.ds(0, 1)], local_sem.at[2 + m])
        )
    for copy in local:
        copy.start()

    barrier = pltpu.get_barrier_semaphore()
    partners = [to_x[1], to_x[2], to_y[1], to_y[2], to_lo, to_hi, to_core]
    for device in partners:
        pl.semaphore_signal(barrier, inc=1, device_id=device, device_id_type=MESH)
    pl.semaphore_wait(barrier, len(partners))

    copies = {}

    def send(name, src, dst, device):
        key = len(copies)
        copies[name] = pltpu.make_async_remote_copy(
            src_ref=src,
            dst_ref=dst,
            send_sem=send_sem.at[key],
            recv_sem=recv_sem.at[key],
            device_id=device,
            device_id_type=MESH,
        )
        copies[name].start()

    def x_direct(s, m):
        src = train_in[m].at[mine] if s == 0 else trains.at[m, 1, 0]
        for place in (1, 2):
            send(("x", s, m, place), src, trains.at[m, s, place], to_x[place])

    def x_forward(s, m, place):
        half = pl.ds(place - 1, 1)
        send(("x", s, m, 3, place), trains.at[m, s, place, half], trains.at[m, s, 3, half], to_x[place])

    def y_direct(s, w, m):
        if (s, w, m) == (0, 1, 1):
            return
        src = val_in[m] if (s, w) == (0, 0) else vals.at[m, s, 0, pl.ds(w, 1)]
        for place in (1, 2):
            send(("y", s, w, m, place), src, vals.at[m, s, place, pl.ds(w, 1)], to_y[place])

    def y_forward(s, w, m, place):
        half = pl.ds((place - 1) * (seq_len // 2), seq_len // 2)
        send(
            ("y", s, w, m, 3, place),
            vals.at[m, s, place, w, half],
            vals.at[m, s, 3, w, half],
            to_y[place],
        )

    def z_share(m, place):
        send(("zs", m, place), vals.at[m, 1, place, 0], vals.at[m, 0, place, 1], to_hi)

    def core_copy(b, v):
        return pltpu.make_async_remote_copy(
            src_ref=grams.at[0, b, v],
            dst_ref=from_core.at[b, v],
            send_sem=core_send_sem.at[b, v],
            recv_sem=core_recv_sem.at[b, v],
            device_id=to_core,
            device_id_type=MESH,
        )

    def gram(s, m, blocks, val_blocks):
        def one(i, carry):
            b, v = blocks[0] + i // len(val_blocks), val_blocks[0] + i % len(val_blocks)
            part = lax.dot_general(
                trains[m, s, b].reshape(2 * seq_len, -1),
                vals[m, s, v].reshape(2 * seq_len, -1),
                (((1,), (1,)), ((), ())),
                preferred_element_type=jnp.float32,
            )
            if s == 0:
                grams[m, b, v] = part
            elif m == 0:
                grams[0, b, v] += part
                core_copy(b, v).start()
            else:
                core_copy(b, v).wait_recv()
                product = (grams[1, b, v] + part) * (grams[0, b, v] + from_core[b, v])
                sums[v, b] = jnp.sum(product.reshape(2, seq_len, 2 * seq_len), axis=1)
            return carry

        lax.fori_loop(0, len(blocks) * len(val_blocks), one, 0)

    group = ((z_lo, core), (z_lo, 1 - core), (1 - z_lo, core), (1 - z_lo, 1 - core))

    def out(blocks):
        first, last = blocks[0], blocks[-1] + 1
        lane = lax.broadcasted_iota(jnp.int32, (last - first, 2, 128), 2)
        scores = jnp.zeros(lane.shape, jnp.float32)
        for v in range(RING):
            for w in range(2):
                part = sums[v, first:last, :, w * seq_len : (w + 1) * seq_len]
                column = (z_hi if w == 0 else 1 - z_hi) * 16 + y_at[v] * 4 + x
                scores = jnp.where(lane == column, jnp.sum(part, axis=2, keepdims=True), scores)
        scores = scores * (1.0 / (total_width * seq_len))
        row = lax.broadcasted_iota(jnp.int32, (8, 128), 0)
        for b in blocks:
            tile = jnp.zeros((8, 128), jnp.float32)
            for r in range(2):
                tile = jnp.where(row == 2 * z_lo + r, scores[b - first, r : r + 1], tile)
            tiles[b] = tile
            for d, (its_z_lo, its_core) in enumerate(group):
                if (b, d) != (0, 0):
                    device = at(z_hi, y, x_at[b], its_z_lo, its_core)
                    send(("out", b, d), tiles.at[b], arrived.at[b, d], device)

    for m in range(2):
        x_direct(0, m)
        y_direct(0, 0, m)
        send(("hi", m), val_in[m], vals.at[m, 1, 0, pl.ds(1, 1)], to_hi)
        send(("lo", m), val_in[m], vals.at[m, 1, 0, pl.ds(0, 1)], to_lo)
    for m in range(2):
        send(("swap", m), train_in[m].at[theirs], trains.at[m, 1, 0], to_lo)
    for copy in local:
        copy.wait()

    far = set()
    for event in ORDER:
        kind = event[0]
        if kind == "gram":
            gram(event[1], event[2], PLACES[event[3]], VALS[event[4]])
            continue
        if kind == "out":
            out(PLACES[event[1]])
            continue
        copies[event].wait_recv()
        if kind == "hi":
            y_direct(1, 1, event[1])
        elif kind == "lo":
            m = event[1]
            send(("far", m), vals.at[m, 1, 0, pl.ds(0, 1)], vals.at[m, 0, 0, pl.ds(1, 1)], to_hi)
            y_direct(1, 0, m)
        elif kind == "far":
            y_direct(0, 1, event[1])
        elif kind == "swap":
            x_direct(1, event[1])
        elif kind == "x" and event[3] < 3:
            x_forward(*event[1:])
        elif kind == "y":
            s, w, m, place = event[1:5]
            if place < 3:
                y_forward(s, w, m, place)
            shared = (s, w, m) == (1, 0, 1)
            if shared and (place < 3 or event[:5] in far):
                z_share(m, place)
            if place == 3:
                far.add(event[:5])

    total = tiles[0]
    for b in range(RING):
        for d in range(4):
            if (b, d) != (0, 0):
                copies["out", b, d].wait_recv()
                total = total + arrived[b, d]
    out_ref[...] = total[: out_ref.shape[0], : out_ref.shape[1]]
    for copy in copies.values():
        copy.wait_send()
    for b in range(RING):
        for v in range(RING):
            core_copy(b, v).wait_send()


N_COPIES = 4 * 4 + 7 * 4 + (6 + 2 + 3) + 15


def per_device(train_act, train_grad, val_act, val_grad):
    n_train, seq_len, width = train_act.shape
    n_val = lax.axis_size("dp")
    bf16, f32 = train_act.dtype, jnp.float32
    anywhere = pl.BlockSpec(memory_space=pl.ANY)
    return pl.pallas_call(
        functools.partial(kernel, width * lax.axis_size("tensor")),
        out_shape=jax.ShapeDtypeStruct((n_train, n_val), f32),
        in_specs=[anywhere] * 4,
        out_specs=pl.BlockSpec(memory_space=pltpu.VMEM),
        scratch_shapes=[
            pltpu.VMEM((2, 2, RING, 2, seq_len, width), bf16),
            pltpu.VMEM((2, 2, RING, 2, seq_len, width), bf16),
            pltpu.VMEM((2, RING, RING, 2 * seq_len, 2 * seq_len), f32),
            pltpu.VMEM((RING, RING, 2 * seq_len, 2 * seq_len), f32),
            pltpu.VMEM((RING, RING, 2, 2 * seq_len), f32),
            pltpu.VMEM((RING, 8, 128), f32),
            pltpu.VMEM((RING, 4, 8, 128), f32),
            pltpu.SemaphoreType.DMA((4,)),
            pltpu.SemaphoreType.DMA((N_COPIES,)),
            pltpu.SemaphoreType.DMA((N_COPIES,)),
            pltpu.SemaphoreType.DMA((RING, RING)),
            pltpu.SemaphoreType.DMA((RING, RING)),
        ],
        compiler_params=pltpu.CompilerParams(
            collective_id=0, has_side_effects=True, vmem_limit_bytes=56 * 1024 * 1024
        ),
        cost_estimate=pl.CostEstimate(
            flops=4 * 64 * (2 * seq_len) ** 2 * width, bytes_accessed=3_300_000, transcendentals=0
        ),
    )(train_act, train_grad, val_act, val_grad)


def solution(mesh):
    placed = P("dp", None, "tensor")
    return jax.shard_map(
        per_device, mesh=mesh, in_specs=(placed,) * 4, out_specs=P("dp", None), check_vma=False
    )
```

time: 117 us -> 102 us (0.87)
  Pallas kernels: 115 us -> 101 us
    pallas_call x1, Pallas kernels: 115 us -> 101 us  [per_device(): pl.pallas_call(functools.partial(kernel, width * lax.axis_size('tensor'))...]
where the time goes in v3:
time: 102 us
  Pallas kernels  101 us (99%)
  local copies, waits for them, and re-layouts  1.26 us (1%)
    pallas_call x1, Pallas kernels, per_device(): pl.pallas_call(functools.partial(kernel, width * lax.axis_size('tensor'))...  101 us

profile of v3, /device:TPU:1, one launch (start us, length us, event | category | flops | bytes accessed | tf_op | source)
XLA Modules:
  0.0 101.9 jit_solution(3259202563975557316)
XLA Ops:
  0.0 100.6 %shard_map.46 = f32[4,32]{1,0:T(4,128)} custom-call(bf16[4,128,1280]{2,1,0:T(8,128)(2,1)} %train_act.1, bf16[4,128,1280]{2,1,0:T(8,128)(2,1)} %train_grad.1, bf16[1,128,1280]{2,1,0:T(8,128)(2,1)} %val_act.1, bf16[1,128,1280]{2,1,0:T(8,128)(2,1)} %val_grad.1), custom_call_target="tpu_custom_call" | custom-call | flops 21474836480 | bytes 3300000 | tf_op jit(solution)/shard_map/pallas_call | solution.py:258
  100.6 1.3 %copy.6 = f32[4,32]{1,0:T(4,128)} copy(f32[4,32]{1,0:T(4,128)} %shard_map.46) | data formatting | bytes 1024

commit v4 on v3

v4 whole, which is shorter than its diff:
```python
import functools

import jax
import jax.numpy as jnp
from jax import lax
from jax.experimental import pallas as pl
from jax.experimental.pallas import tpu as pltpu
from jax.sharding import PartitionSpec as P

MESH = pl.DeviceIdType.MESH
RING = 4

BLOCKS = {"o": (0, 1), "p": (2, 3)}
PLACES = {"a": (0,), "b": (1, 2), "c": (3,), "d": (4,), "e": (5, 6), "f": (7,)}

ORDER = (
    ("s1", "o", "a", 0), ("s2", "o", "a", 0), ("ra", 0), ("rb", 0), ("y", 0, 0, 0, 1), ("y", 0, 0, 0, 2),
    ("v", 0, 0, 0), ("ra", 1), ("rb", 1), ("s1", "o", "b", 0), ("s3", "o", "a", 0), ("s1", "o", "d", 0),
    ("s2", "o", "b", 0), ("fa", 0), ("s2", "o", "d", 0), ("fb", 0), ("s1", "o", "a", 1), ("x", 0, 0),
    ("y", 0, 0, 1, 1), ("y", 0, 0, 1, 2), ("v", 0, 1, 0), ("fa", 1), ("s2", "o", "a", 1), ("fb", 1),
    ("y", 0, 0, 0, 3, 1), ("y", 0, 0, 0, 3, 2), ("s1", "o", "c", 0), ("s3", "o", "b", 0), ("s3", "o", "d", 0),
    ("s2", "o", "c", 0), ("v", 0, 0, 1), ("s3", "o", "a", 1), ("s4", "o", "a"), ("s3", "o", "c", 0),
    ("y", 0, 1, 0, 1), ("y", 0, 1, 0, 2), ("s1", "o", "b", 1), ("s2", "o", "b", 1), ("x", 0, 1),
    ("v", 0, 0, 2), ("y", 0, 0, 1, 3, 1), ("y", 0, 0, 1, 3, 2), ("s1", "p", "a", 0), ("s1", "p", "b", 0),
    ("s1", "p", "c", 0), ("s1", "p", "d", 0), ("s1", "o", "e", 0), ("s2", "p", "a", 0), ("s2", "p", "b", 0),
    ("s2", "p", "c", 0), ("s1", "p", "e", 0), ("s2", "p", "d", 0), ("s2", "o", "e", 0), ("s3", "o", "b", 1),
    ("s1", "p", "a", 1), ("s1", "p", "b", 1), ("v", 1, 0, 0), ("y", 0, 1, 1, 1), ("y", 0, 1, 1, 2),
    ("s2", "p", "e", 0), ("s3", "p", "a", 0), ("s2", "p", "a", 1), ("s1", "o", "d", 1), ("s2", "p", "b", 1),
    ("s1", "p", "d", 1), ("s3", "p", "b", 0), ("y", 0, 1, 0, 3, 1), ("y", 0, 1, 0, 3, 2), ("s1", "o", "c", 1),
    ("s2", "o", "d", 1), ("s3", "p", "c", 0), ("s1", "p", "c", 1), ("s2", "p", "d", 1), ("s4", "o", "b"),
    ("x", 1, 0), ("v", 0, 1, 1), ("s2", "o", "c", 1), ("s2", "p", "c", 1), ("s3", "p", "d", 0),
    ("s3", "o", "e", 0), ("y", 1, 1, 0, 1), ("y", 1, 1, 0, 2), ("s1", "o", "e", 1), ("s1", "p", "e", 1),
    ("s3", "p", "e", 0), ("s3", "p", "a", 1), ("s2", "o", "e", 1), ("y", 0, 1, 1, 3, 1), ("y", 0, 1, 1, 3, 2),
    ("v", 0, 1, 2), ("s2", "p", "e", 1), ("s3", "p", "b", 1), ("y", 1, 1, 0, 3, 1), ("y", 1, 1, 0, 3, 2),
    ("s3", "o", "d", 1), ("s1", "o", "f", 1), ("s1", "p", "f", 1), ("s3", "p", "d", 1), ("s2", "o", "f", 1),
    ("s2", "p", "f", 1), ("s3", "o", "c", 1), ("x", 1, 1), ("v", 1, 1, 0), ("s4", "p", "a"),
    ("s3", "p", "c", 1), ("s4", "p", "b"), ("s4", "o", "c"), ("s3", "o", "e", 1), ("s4", "p", "c"),
    ("s4", "o", "d"), ("s4", "p", "d"), ("v", 0, 0, 3), ("s3", "p", "e", 1), ("s1", "o", "f", 0),
    ("s1", "p", "f", 0), ("s3", "o", "f", 1), ("y", 1, 1, 1, 1), ("y", 1, 1, 1, 2), ("s4", "o", "e"),
    ("s2", "o", "f", 0), ("s2", "p", "f", 0), ("s3", "p", "f", 1), ("s4", "p", "e"), ("v", 0, 1, 3),
    ("y", 1, 1, 1, 3, 1), ("y", 1, 1, 1, 3, 2), ("s3", "o", "f", 0), ("s3", "p", "f", 0), ("s4", "o", "f"),
    ("s4", "p", "f"),
)

POWER = 16
PEAK = 222.0


def kernel(
    total_width,
    train_act,
    train_grad,
    val_act,
    val_grad,
    out_ref,
    trains,
    vals,
    relay,
    acts,
    from_core,
    coded_out,
    coded_in,
    whole,
    sums,
    tiles,
    arrived,
    local_sem,
    send_sem,
    recv_sem,
):
    seq_len = train_act.shape[1]
    train_in = (train_act, train_grad)
    val_in = (val_act, val_grad)

    dp = lax.axis_index("dp")
    tensor = lax.axis_index("tensor")
    z_hi, y, x = dp // 16, (dp // 4) % 4, dp % 4
    z_lo, core = tensor // 2, tensor % 2

    def at(z_hi, y, x, z_lo, core):
        return (z_hi * 16 + y * 4 + x, z_lo * 2 + core)

    mate, twin = x + 1 - 2 * (x % 2), 3 - x
    y_at = (y, (y + 3) % 4, (y + 1) % 4, (y + 2) % 4)
    to_y = {1: at(z_hi, y_at[2], x, z_lo, core), 2: at(z_hi, y_at[1], x, z_lo, core)}
    to_mate = at(z_hi, y, mate, z_lo, core)
    to_twin = at(z_hi, y, twin, z_lo, core)
    to_lo = at(z_hi, y, x, 1 - z_lo, core)
    to_hi = at(1 - z_hi, y, x, 1 - z_lo, core)
    to_core = at(z_hi, y, x, z_lo, 1 - core)

    local = []
    for m in range(2):
        local.append(
            pltpu.make_async_copy(train_in[m], trains.at[m, pl.ds(0, 4)], local_sem.at[m])
        )
        local.append(
            pltpu.make_async_copy(val_in[m], vals.at[m, 0, pl.ds(0, 1)], local_sem.at[2 + m])
        )
    for copy in local:
        copy.start()

    barrier = pltpu.get_barrier_semaphore()
    partners = [to_mate, to_twin, to_y[1], to_y[2], to_lo, to_hi, to_core]
    for device in partners:
        pl.semaphore_signal(barrier, inc=1, device_id=device, device_id_type=MESH)
    pl.semaphore_wait(barrier, len(partners))

    copies = {}

    def send(name, src, dst, device):
        key = len(copies)
        copies[name] = pltpu.make_async_remote_copy(
            src_ref=src,
            dst_ref=dst,
            send_sem=send_sem.at[key],
            recv_sem=recv_sem.at[key],
            device_id=device,
            device_id_type=MESH,
        )
        copies[name].start()

    def got(name):
        copies[name].wait_recv()

    def own_val(w, m):
        return val_in[m].at[0] if w == 0 else vals.at[m, 0, 1]

    def y_direct(q, w, m):
        src = own_val(w, m) if q == 0 else vals.at[m, RING, w]
        for place in (1, 2):
            send(("y", q, w, m, place), src, vals.at[m, q * RING + place, w], to_y[place])

    def y_forward(q, w, m, place):
        half = pl.ds((place - 1) * (seq_len // 2), seq_len // 2)
        send(
            ("y", q, w, m, 3, place),
            vals.at[m, q * RING + place, w, half],
            vals.at[m, q * RING + 3, w, half],
            to_y[place],
        )

    def v_direct(w, m, place):
        src = own_val(w, m) if place == 0 else vals.at[m, place, w]
        send(("v", w, m, place), src, vals.at[m, RING + place, w], to_twin)

    def own_ready(w, m):
        y_direct(0, w, m)
        v_direct(w, m, 0)

    def have(q, w, m, place):
        if q == 0 and w == 0 and place > 0:
            v_direct(w, m, place)
        if q == 1 and w == 1 and place == 0:
            y_direct(1, w, m)

    starts, rows = {}, {}
    for event in ORDER:
        if event[0] == "s1":
            size = len(BLOCKS[event[1]]) * len(PLACES[event[2]])
            first = sum(n for _, n in starts.values())
            rows[event[1:]] = (first * seq_len + 16 * len(starts), size * seq_len + 16)
            starts[event[1:]] = (first, size)

    def act_product(group):
        blocks, places, w = BLOCKS[group[0]], PLACES[group[1]], group[2]
        first, size = starts[group]
        n = len(blocks)

        def one(i, carry):
            part = lax.dot_general(
                trains[0, 2 * blocks[0] : 2 * blocks[0] + 2 * n].reshape(2 * n * seq_len, -1),
                vals[0, places[0] + i, w],
                (((1,), (1,)), ((), ())),
                preferred_element_type=jnp.float32,
            )
            for k in range(n):
                for r in range(2):
                    at_row = (2 * k + r) * seq_len
                    acts[r, first + i * n + k] = part[at_row : at_row + seq_len]
            return carry

        lax.fori_loop(0, len(places), one, 0)
        send(("s1",) + group, acts.at[1 - core, pl.ds(first, size)], from_core.at[pl.ds(first, size)], to_core)

    def act_cores(group):
        first, size = starts[group]
        row, n_rows = rows[group]
        got(("s1",) + group)

        def add(i, peak):
            value = acts[core, first + i] + from_core[first + i]
            acts[core, first + i] = value
            return jnp.maximum(peak, jnp.max(jnp.abs(value).reshape(seq_len // 8, 8, seq_len), axis=0))

        peak = lax.fori_loop(0, size, add, jnp.zeros((8, seq_len), jnp.float32))
        peak = jnp.max(jnp.max(peak, axis=0, keepdims=True), axis=1, keepdims=True)
        scale = jnp.broadcast_to(jnp.maximum(peak, 1e-30) * 1.01, (16, seq_len)).astype(jnp.bfloat16)
        coded_out[pl.ds(row + size * seq_len, 16)] = scale
        inverse = PEAK / scale.astype(jnp.float32)[0:1]

        def code(i, carry):
            value = acts[core, first + i]
            power = jnp.abs(value) * inverse
            for _ in range(4):
                power = power * power
            power = jnp.where(value < 0, -power, power).astype(jnp.bfloat16)
            coded_out[pl.ds(pl.multiple_of(row + i * seq_len, 16), seq_len)] = power
            return carry

        lax.fori_loop(0, size, code, 0)
        send(("s2",) + group, coded_out.at[pl.ds(row, n_rows)], coded_in.at[pl.ds(row, n_rows)], to_lo)

    def act_whole(group):
        first, size = starts[group]
        row, _ = rows[group]
        got(("s2",) + group)
        scale = coded_in[pl.ds(row + size * seq_len, 16)].astype(jnp.float32)[0:1] * (1.0 / PEAK)

        def one(i, carry):
            power = coded_in[pl.ds(pl.multiple_of(row + i * seq_len, 16), seq_len)].astype(jnp.float32)
            size_of = jnp.abs(power)
            value = jnp.exp(jnp.log(size_of) * (1.0 / POWER)) * scale
            value = jnp.where(power < 0, -value, value)
            whole[core, first + i] = acts[core, first + i] + jnp.where(size_of > 0, value, 0.0)
            return carry

        lax.fori_loop(0, size, one, 0)
        here = whole.at[core, pl.ds(first, size)]
        send(("s3",) + group, here, here, to_core)

    def grad_product(b_key, p_key):
        blocks, places = BLOCKS[b_key], PLACES[p_key]
        n = len(blocks)
        for w in range(2):
            got(("s3", b_key, p_key, w))

        def one(i, carry):
            v, b = places[0] + i // n, blocks[0] + i % n
            part = lax.dot_general(
                trains[1, pl.ds(2 * b, 2)].reshape(2 * seq_len, -1),
                vals[1, v].reshape(2 * seq_len, -1),
                (((1,), (1,)), ((), ())),
                preferred_element_type=jnp.float32,
            )
            for r in range(2):
                for w in range(2):
                    act = whole[r, starts[b_key, p_key, w][0] + i]
                    grad = part[r * seq_len : (r + 1) * seq_len, w * seq_len : (w + 1) * seq_len]
                    sums[v, w, b, r : r + 1] = jnp.sum(act * grad, axis=0, keepdims=True)
            return carry

        lax.fori_loop(0, n * len(places), one, 0)

    group_of = ((z_lo, core), (z_lo, 1 - core), (1 - z_lo, core), (1 - z_lo, 1 - core))

    def out():
        lane = lax.broadcasted_iota(jnp.int32, (RING, 2, 128), 2)
        scores = jnp.zeros(lane.shape, jnp.float32)
        for v in range(2 * RING):
            for w in range(2):
                its_z_hi = z_hi if w == 0 else 1 - z_hi
                column = its_z_hi * 16 + y_at[v % RING] * 4 + (x if v < RING else twin)
                scores = jnp.where(lane == column, jnp.sum(sums[v, w], axis=2, keepdims=True), scores)
        scores = scores * (1.0 / (total_width * seq_len))
        tiles[...] = jnp.zeros_like(tiles)
        for b in range(RING):
            for r in range(2):
                at_row = (b % 2) * 2 + r
                tiles[b // 2, at_row : at_row + 1] = scores[b, r : r + 1]
        for side, its_x in ((1, mate), (0, x)):
            for d, (its_z_lo, its_core) in enumerate(group_of):
                if (side, d) != (0, 0):
                    device = at(z_hi, y, its_x, its_z_lo, its_core)
                    send(("out", side, d), tiles.at[side], arrived.at[side, d], device)

    half_a, half_b = pl.ds(0, seq_len // 2), pl.ds(seq_len // 2, seq_len // 2)
    for m in range(2):
        send(("ra", m), val_in[m].at[0, half_a], relay.at[0, m], to_lo)
        send(("rb", m), val_in[m].at[0, half_b], relay.at[1, m], to_hi)
        for h in range(2):
            send(("x", m, h), train_in[m].at[pl.ds(2 * h, 2)], trains.at[m, pl.ds(4 + 2 * h, 2)], to_mate)
        own_ready(0, m)
    for copy in local:
        copy.wait()

    seen = set()
    for event in ORDER:
        kind = event[0]
        if kind == "s1":
            act_product(event[1:])
            continue
        if kind == "s2":
            act_cores(event[1:])
            continue
        if kind == "s3":
            act_whole(event[1:])
            continue
        if kind == "s4":
            grad_product(*event[1:])
            continue
        got(event)
        if kind == "ra":
            m = event[1]
            send(("fa", m), relay.at[0, m], vals.at[m, 0, 1, half_a], to_hi)
        elif kind == "rb":
            m = event[1]
            send(("fb", m), relay.at[1, m], vals.at[m, 0, 1, half_b], to_lo)
        elif kind in ("fa", "fb"):
            m = event[1]
            if ("f", m) in seen:
                own_ready(1, m)
            seen.add(("f", m))
        elif kind == "v":
            have(1, *event[1:])
        elif kind == "y":
            q, w, m, place = event[1:5]
            if place < 3:
                y_forward(q, w, m, place)
                have(q, w, m, place)
            elif event[:5] in seen:
                have(q, w, m, place)
            seen.add(event[:5])
    out()

    total = tiles[0]
    for side in range(2):
        for d in range(4):
            if (side, d) != (0, 0):
                got(("out", side, d))
                total = total + arrived[side, d]
    out_ref[...] = total[: out_ref.shape[0], : out_ref.shape[1]]
    for copy in copies.values():
        copy.wait_send()


GROUPS = 2 * len(BLOCKS) * len(PLACES)
UNITS = 2 * 4 * 2 * RING
N_COPIES = 8 + 4 + 2 * 3 * 4 + 2 * (RING + 1) + 3 * GROUPS + 7


def per_device(train_act, train_grad, val_act, val_grad):
    n_train, seq_len, width = train_act.shape
    n_val = lax.axis_size("dp")
    bf16, f32 = train_act.dtype, jnp.float32
    anywhere = pl.BlockSpec(memory_space=pl.ANY)
    coded = (UNITS * seq_len + 16 * GROUPS, seq_len)
    return pl.pallas_call(
        functools.partial(kernel, width * lax.axis_size("tensor")),
        out_shape=jax.ShapeDtypeStruct((n_train, n_val), f32),
        in_specs=[anywhere] * 4,
        out_specs=pl.BlockSpec(memory_space=pltpu.VMEM),
        scratch_shapes=[
            pltpu.VMEM((2, 2 * n_train, seq_len, width), bf16),
            pltpu.VMEM((2, 2 * RING, 2, seq_len, width), bf16),
            pltpu.VMEM((2, 2, seq_len // 2, width), bf16),
            pltpu.VMEM((2, UNITS, seq_len, seq_len), f32),
            pltpu.VMEM((UNITS, seq_len, seq_len), f32),
            pltpu.VMEM(coded, bf16),
            pltpu.VMEM(coded, bf16),
            pltpu.VMEM((2, UNITS, seq_len, seq_len), f32),
            pltpu.VMEM((2 * RING, 2, RING, 2, seq_len), f32),
            pltpu.VMEM((2, 8, 128), f32),
            pltpu.VMEM((2, 4, 8, 128), f32),
            pltpu.SemaphoreType.DMA((4,)),
            pltpu.SemaphoreType.DMA((N_COPIES,)),
            pltpu.SemaphoreType.DMA((N_COPIES,)),
        ],
        compiler_params=pltpu.CompilerParams(
            collective_id=0, has_side_effects=True, vmem_limit_bytes=56 * 1024 * 1024
        ),
        cost_estimate=pl.CostEstimate(
            flops=4 * 32 * (2 * seq_len) ** 2 * width, bytes_accessed=3_300_000, transcendentals=0
        ),
    )(train_act, train_grad, val_act, val_grad)


def solution(mesh):
    placed = P("dp", None, "tensor")
    return jax.shard_map(
        per_device, mesh=mesh, in_specs=(placed,) * 4, out_specs=P("dp", None), check_vma=False
    )
```

time: 102 us -> 92.4 us (0.906)
  Pallas kernels: 101 us -> 91.1 us
    pallas_call x1, Pallas kernels: 101 us -> 91.1 us  [per_device(): pl.pallas_call(functools.partial(kernel, width * lax.axis_size('tensor'))...]
where the time goes in v4:
time: 92.4 us; the launch traced here: 92.3 us
  Pallas kernels  91.1 us (99%)
  local copies, waits for them, and re-layouts  1.26 us (1%)
    pallas_call x1, Pallas kernels, per_device(): pl.pallas_call(functools.partial(kernel, width * lax.axis_size('tensor'))...  91.1 us

profile of v4, /device:TPU:1, one launch (start us, length us, event | category | flops | bytes accessed | tf_op | source)
XLA Modules:
  0.0 92.3 jit_solution(9981684423065317172)
XLA Ops:
  0.0 91.1 %shard_map.46 = f32[4,32]{1,0:T(4,128)} custom-call(bf16[4,128,1280]{2,1,0:T(8,128)(2,1)} %train_act.1, bf16[4,128,1280]{2,1,0:T(8,128)(2,1)} %train_grad.1, bf16[1,128,1280]{2,1,0:T(8,128)(2,1)} %val_act.1, bf16[1,128,1280]{2,1,0:T(8,128)(2,1)} %val_grad.1), custom_call_target="tpu_custom_call" | custom-call | flops 10737418240 | bytes 3300000 | tf_op jit(solution)/shard_map/pallas_call | solution.py:348
  91.1 1.3 %copy.6 = f32[4,32]{1,0:T(4,128)} copy(f32[4,32]{1,0:T(4,128)} %shard_map.46) | data formatting | bytes 1024

commit v5 on v4

--- a/solution.py
+++ b/solution.py
@@ -10,36 +10,53 @@
 MESH = pl.DeviceIdType.MESH
 RING = 4
 
-BLOCKS = {"o": (0, 1), "p": (2, 3)}
+BLOCKS = {"o": (0, 1), "p": (2,), "s": (3,)}
 PLACES = {"a": (0,), "b": (1, 2), "c": (3,), "d": (4,), "e": (5, 6), "f": (7,)}
 
+PIECES = (
+    (0, 0, 0, 32, "v"),
+    (0, 0, 32, 96, "y"),
+    (1, 0, 0, 128, "v"),
+    (0, 1, 0, 128, "y"),
+    (1, 1, 0, 128, "v"),
+)
+
 ORDER = (
-    ("s1", "o", "a", 0), ("s2", "o", "a", 0), ("ra", 0), ("rb", 0), ("y", 0, 0, 0, 1), ("y", 0, 0, 0, 2),
-    ("v", 0, 0, 0), ("ra", 1), ("rb", 1), ("s1", "o", "b", 0), ("s3", "o", "a", 0), ("s1", "o", "d", 0),
-    ("s2", "o", "b", 0), ("fa", 0), ("s2", "o", "d", 0), ("fb", 0), ("s1", "o", "a", 1), ("x", 0, 0),
-    ("y", 0, 0, 1, 1), ("y", 0, 0, 1, 2), ("v", 0, 1, 0), ("fa", 1), ("s2", "o", "a", 1), ("fb", 1),
-    ("y", 0, 0, 0, 3, 1), ("y", 0, 0, 0, 3, 2), ("s1", "o", "c", 0), ("s3", "o", "b", 0), ("s3", "o", "d", 0),
-    ("s2", "o", "c", 0), ("v", 0, 0, 1), ("s3", "o", "a", 1), ("s4", "o", "a"), ("s3", "o", "c", 0),
-    ("y", 0, 1, 0, 1), ("y", 0, 1, 0, 2), ("s1", "o", "b", 1), ("s2", "o", "b", 1), ("x", 0, 1),
-    ("v", 0, 0, 2), ("y", 0, 0, 1, 3, 1), ("y", 0, 0, 1, 3, 2), ("s1", "p", "a", 0), ("s1", "p", "b", 0),
-    ("s1", "p", "c", 0), ("s1", "p", "d", 0), ("s1", "o", "e", 0), ("s2", "p", "a", 0), ("s2", "p", "b", 0),
-    ("s2", "p", "c", 0), ("s1", "p", "e", 0), ("s2", "p", "d", 0), ("s2", "o", "e", 0), ("s3", "o", "b", 1),
-    ("s1", "p", "a", 1), ("s1", "p", "b", 1), ("v", 1, 0, 0), ("y", 0, 1, 1, 1), ("y", 0, 1, 1, 2),
-    ("s2", "p", "e", 0), ("s3", "p", "a", 0), ("s2", "p", "a", 1), ("s1", "o", "d", 1), ("s2", "p", "b", 1),
-    ("s1", "p", "d", 1), ("s3", "p", "b", 0), ("y", 0, 1, 0, 3, 1), ("y", 0, 1, 0, 3, 2), ("s1", "o", "c", 1),
-    ("s2", "o", "d", 1), ("s3", "p", "c", 0), ("s1", "p", "c", 1), ("s2", "p", "d", 1), ("s4", "o", "b"),
-    ("x", 1, 0), ("v", 0, 1, 1), ("s2", "o", "c", 1), ("s2", "p", "c", 1), ("s3", "p", "d", 0),
-    ("s3", "o", "e", 0), ("y", 1, 1, 0, 1), ("y", 1, 1, 0, 2), ("s1", "o", "e", 1), ("s1", "p", "e", 1),
-    ("s3", "p", "e", 0), ("s3", "p", "a", 1), ("s2", "o", "e", 1), ("y", 0, 1, 1, 3, 1), ("y", 0, 1, 1, 3, 2),
-    ("v", 0, 1, 2), ("s2", "p", "e", 1), ("s3", "p", "b", 1), ("y", 1, 1, 0, 3, 1), ("y", 1, 1, 0, 3, 2),
-    ("s3", "o", "d", 1), ("s1", "o", "f", 1), ("s1", "p", "f", 1), ("s3", "p", "d", 1), ("s2", "o", "f", 1),
-    ("s2", "p", "f", 1), ("s3", "o", "c", 1), ("x", 1, 1), ("v", 1, 1, 0), ("s4", "p", "a"),
-    ("s3", "p", "c", 1), ("s4", "p", "b"), ("s4", "o", "c"), ("s3", "o", "e", 1), ("s4", "p", "c"),
-    ("s4", "o", "d"), ("s4", "p", "d"), ("v", 0, 0, 3), ("s3", "p", "e", 1), ("s1", "o", "f", 0),
-    ("s1", "p", "f", 0), ("s3", "o", "f", 1), ("y", 1, 1, 1, 1), ("y", 1, 1, 1, 2), ("s4", "o", "e"),
-    ("s2", "o", "f", 0), ("s2", "p", "f", 0), ("s3", "p", "f", 1), ("s4", "p", "e"), ("v", 0, 1, 3),
-    ("y", 1, 1, 1, 3, 1), ("y", 1, 1, 1, 3, 2), ("s3", "o", "f", 0), ("s3", "p", "f", 0), ("s4", "o", "f"),
-    ("s4", "p", "f"),
+    ("s1", "o", "a", 0), ("s2", "o", "a", 0), ("v", 0, 0), ("y", 0, 0, 1), ("y", 0, 0, 2), ("ra", 0),
+    ("rb", 0), ("v", 1, 0), ("y", 0, 1, 1), ("y", 0, 1, 2), ("ra", 1), ("rb", 1), ("s1", "o", "b", 0),
+    ("s3", "o", "a", 0), ("s1", "o", "d", 0), ("s2", "o", "b", 0), ("fa", 0), ("s2", "o", "d", 0), ("fb", 0),
+    ("s1", "o", "a", 1), ("v", 3, 0), ("y", 0, 3, 1), ("y", 0, 3, 2), ("x", 0, 0), ("fa", 1),
+    ("s2", "o", "a", 1), ("s1", "p", "a", 0), ("s1", "p", "b", 0), ("fb", 1), ("s1", "p", "d", 0),
+    ("y", 1, 0, 1), ("y", 1, 0, 2), ("s1", "p", "a", 1), ("y", 0, 0, 3, 1), ("y", 0, 0, 3, 2),
+    ("s2", "p", "a", 0), ("s2", "p", "b", 0), ("s2", "p", "d", 0), ("s2", "p", "a", 1), ("s3", "o", "b", 0),
+    ("y", 0, 1, 3, 1), ("v", 1, 1), ("y", 0, 1, 3, 2), ("s1", "o", "c", 0), ("s3", "o", "d", 0),
+    ("s1", "p", "c", 0), ("s3", "o", "a", 1), ("s2", "o", "c", 0), ("s3", "p", "a", 0), ("s2", "p", "c", 0),
+    ("s4", "o", "a"), ("s3", "p", "b", 0), ("v", 1, 2), ("s3", "p", "d", 0), ("s1", "o", "e", 0),
+    ("s3", "p", "a", 1), ("s1", "p", "e", 0), ("y", 0, 2, 1), ("y", 0, 2, 2), ("s1", "o", "b", 1),
+    ("s3", "o", "c", 0), ("s2", "o", "e", 0), ("x", 0, 1), ("s2", "p", "e", 0), ("s3", "p", "c", 0),
+    ("s1", "s", "a", 0), ("s1", "s", "b", 0), ("s2", "o", "b", 1), ("s1", "s", "c", 0), ("y", 0, 3, 3, 1),
+    ("y", 0, 3, 3, 2), ("s1", "s", "d", 0), ("s1", "s", "e", 0), ("s2", "s", "a", 0), ("s1", "s", "a", 1),
+    ("s2", "s", "b", 0), ("s1", "p", "b", 1), ("v", 2, 0), ("s2", "s", "c", 0), ("s1", "s", "b", 1),
+    ("s2", "s", "d", 0), ("s1", "o", "d", 1), ("s2", "s", "e", 0), ("s2", "s", "a", 1), ("s3", "o", "e", 0),
+    ("s2", "p", "b", 1), ("s1", "p", "d", 1), ("s2", "s", "b", 1), ("s3", "p", "e", 0), ("s2", "o", "d", 1),
+    ("s1", "s", "d", 1), ("s2", "p", "d", 1), ("y", 0, 4, 1), ("y", 0, 4, 2), ("s2", "s", "d", 1),
+    ("s3", "o", "b", 1), ("y", 1, 0, 3, 1), ("y", 1, 0, 3, 2), ("s3", "s", "a", 0), ("v", 3, 1),
+    ("s3", "s", "b", 0), ("s4", "o", "b"), ("y", 0, 2, 3, 1), ("y", 0, 2, 3, 2), ("s3", "s", "c", 0),
+    ("x", 1, 0), ("s3", "s", "d", 0), ("s1", "o", "c", 1), ("s3", "s", "e", 0), ("s1", "p", "c", 1),
+    ("s1", "s", "c", 1), ("s4", "p", "a"), ("s3", "s", "a", 1), ("s2", "o", "c", 1), ("s3", "p", "b", 1),
+    ("s2", "p", "c", 1), ("s2", "s", "c", 1), ("v", 3, 2), ("s3", "s", "b", 1), ("s4", "p", "b"),
+    ("s3", "o", "d", 1), ("y", 1, 2, 1), ("y", 1, 2, 2), ("s1", "o", "e", 1), ("s3", "p", "d", 1),
+    ("s1", "p", "e", 1), ("s3", "s", "d", 1), ("s1", "s", "e", 1), ("s3", "o", "c", 1), ("s2", "o", "e", 1),
+    ("y", 0, 4, 3, 1), ("y", 0, 4, 3, 2), ("s2", "p", "e", 1), ("s2", "s", "e", 1), ("s3", "p", "c", 1),
+    ("v", 4, 0), ("s3", "s", "c", 1), ("s4", "o", "d"), ("s4", "o", "c"), ("s4", "p", "c"), ("y", 1, 2, 3, 1),
+    ("y", 1, 2, 3, 2), ("s1", "o", "f", 1), ("s1", "p", "f", 1), ("x", 1, 1), ("s1", "s", "f", 1),
+    ("s4", "p", "d"), ("s3", "o", "e", 1), ("s4", "s", "a"), ("v", 1, 3), ("s2", "o", "f", 1),
+    ("s2", "p", "f", 1), ("s2", "s", "f", 1), ("s3", "p", "e", 1), ("s1", "o", "f", 0), ("s1", "p", "f", 0),
+    ("s1", "s", "f", 0), ("s4", "s", "b"), ("s3", "s", "e", 1), ("s4", "s", "c"), ("s2", "o", "f", 0),
+    ("s2", "p", "f", 0), ("s2", "s", "f", 0), ("s4", "s", "d"), ("s3", "o", "f", 1), ("y", 1, 4, 1),
+    ("y", 1, 4, 2), ("s3", "p", "f", 1), ("s4", "o", "e"), ("s3", "s", "f", 1), ("s4", "p", "e"), ("v", 3, 3),
+    ("s3", "o", "f", 0), ("s3", "p", "f", 0), ("s4", "s", "e"), ("s3", "s", "f", 0), ("y", 1, 4, 3, 1),
+    ("y", 1, 4, 3, 2), ("s4", "o", "f"), ("s4", "p", "f"), ("s4", "s", "f"),
 )
 
 POWER = 16
@@ -123,36 +140,45 @@
     def got(name):
         copies[name].wait_recv()
 
-    def own_val(w, m):
-        return val_in[m].at[0] if w == 0 else vals.at[m, 0, 1]
-
-    def y_direct(q, w, m):
-        src = own_val(w, m) if q == 0 else vals.at[m, RING, w]
+    def own_val(piece):
+        w, m, row, rows, _ = PIECES[piece]
+        rows = pl.ds(row, rows)
+        return val_in[m].at[0, rows] if w == 0 else vals.at[m, 0, 1, rows]
+
+    def y_direct(q, piece):
+        w, m, row, rows, _ = PIECES[piece]
+        src = own_val(piece) if q == 0 else vals.at[m, RING, w, pl.ds(row, rows)]
         for place in (1, 2):
-            send(("y", q, w, m, place), src, vals.at[m, q * RING + place, w], to_y[place])
-
-    def y_forward(q, w, m, place):
-        half = pl.ds((place - 1) * (seq_len // 2), seq_len // 2)
+            dst = vals.at[m, q * RING + place, w, pl.ds(row, rows)]
+            send(("y", q, piece, place), src, dst, to_y[place])
+
+    def y_forward(q, piece, place):
+        w, m, row, rows, _ = PIECES[piece]
+        half = pl.ds(row + (place - 1) * (rows // 2), rows // 2)
         send(
-            ("y", q, w, m, 3, place),
+            ("y", q, piece, 3, place),
             vals.at[m, q * RING + place, w, half],
             vals.at[m, q * RING + 3, w, half],
             to_y[place],
         )
 
-    def v_direct(w, m, place):
-        src = own_val(w, m) if place == 0 else vals.at[m, place, w]
-        send(("v", w, m, place), src, vals.at[m, RING + place, w], to_twin)
+    def v_direct(piece, place):
+        w, m, row, rows, _ = PIECES[piece]
+        src = own_val(piece) if place == 0 else vals.at[m, place, w, pl.ds(row, rows)]
+        send(("v", piece, place), src, vals.at[m, RING + place, w, pl.ds(row, rows)], to_twin)
 
     def own_ready(w, m):
-        y_direct(0, w, m)
-        v_direct(w, m, 0)
-
-    def have(q, w, m, place):
-        if q == 0 and w == 0 and place > 0:
-            v_direct(w, m, place)
-        if q == 1 and w == 1 and place == 0:
-            y_direct(1, w, m)
+        for piece, what in enumerate(PIECES):
+            if what[:2] == (w, m):
+                v_direct(piece, 0)
+                y_direct(0, piece)
+
+    def have(q, piece, place):
+        first = PIECES[piece][4]
+        if first == "y" and q == 0 and place > 0:
+            v_direct(piece, place)
+        if first == "v" and q == 1 and place == 0:
+            y_direct(1, piece)
 
     starts, rows = {}, {}
     for event in ORDER:
@@ -275,12 +301,17 @@
                     send(("out", side, d), tiles.at[side], arrived.at[side, d], device)
 
     half_a, half_b = pl.ds(0, seq_len // 2), pl.ds(seq_len // 2, seq_len // 2)
-    for m in range(2):
+    def pass_on(m):
         send(("ra", m), val_in[m].at[0, half_a], relay.at[0, m], to_lo)
         send(("rb", m), val_in[m].at[0, half_b], relay.at[1, m], to_hi)
+
+    own_ready(0, 0)
+    pass_on(0)
+    pass_on(1)
+    own_ready(0, 1)
+    for m in range(2):
         for h in range(2):
             send(("x", m, h), train_in[m].at[pl.ds(2 * h, 2)], trains.at[m, pl.ds(4 + 2 * h, 2)], to_mate)
-        own_ready(0, m)
     for copy in local:
         copy.wait()
 
@@ -314,13 +345,13 @@
         elif kind == "v":
             have(1, *event[1:])
         elif kind == "y":
-            q, w, m, place = event[1:5]
+            q, piece, place = event[1:4]
             if place < 3:
-                y_forward(q, w, m, place)
-                have(q, w, m, place)
-            elif event[:5] in seen:
-                have(q, w, m, place)
-            seen.add(event[:5])
+                y_forward(q, piece, place)
+                have(q, piece, place)
+            elif event[:4] in seen:
+                have(q, piece, place)
+            seen.add(event[:4])
     out()
 
     total = tiles[0]
@@ -336,7 +367,9 @@
 
 GROUPS = 2 * len(BLOCKS) * len(PLACES)
 UNITS = 2 * 4 * 2 * RING
-N_COPIES = 8 + 4 + 2 * 3 * 4 + 2 * (RING + 1) + 3 * GROUPS + 7
+Y_RINGS = sum(1 if first == "y" else 2 for *_, first in PIECES)
+V_COPIES = sum(RING if first == "y" else 1 for *_, first in PIECES)
+N_COPIES = 8 + 4 + 4 * Y_RINGS + V_COPIES + 3 * GROUPS + 7
 
 
 def per_device(train_act, train_grad, val_act, val_grad):

time: 92.4 us -> 89 us (0.963)
  Pallas kernels: 91.1 us -> 87.6 us
    pallas_call x1, Pallas kernels: 91.1 us -> 87.6 us  [per_device(): pl.pallas_call(functools.partial(kernel, width * lax.axis_size('tensor'))...]
where the time goes in v5:
time: 89 us; the launch traced here: 88.8 us
  Pallas kernels  87.6 us (98%)
  local copies, waits for them, and re-layouts  1.26 us (1%)
    pallas_call x1, Pallas kernels, per_device(): pl.pallas_call(functools.partial(kernel, width * lax.axis_size('tensor'))...  87.6 us

profile of v5, /device:TPU:1, one launch (start us, length us, event | category | flops | bytes accessed | tf_op | source)
XLA Modules:
  0.0 88.8 jit_solution(14923604274396825077)
XLA Ops:
  0.0 87.6 %shard_map.46 = f32[4,32]{1,0:T(4,128)} custom-call(bf16[4,128,1280]{2,1,0:T(8,128)(2,1)} %train_act.1, bf16[4,128,1280]{2,1,0:T(8,128)(2,1)} %train_grad.1, bf16[1,128,1280]{2,1,0:T(8,128)(2,1)} %val_act.1, bf16[1,128,1280]{2,1,0:T(8,128)(2,1)} %val_grad.1), custom_call_target="tpu_custom_call" | custom-call | flops 10737418240 | bytes 3300000 | tf_op jit(solution)/shard_map/pallas_call | solution.py:381
  87.6 1.3 %copy.6 = f32[4,32]{1,0:T(4,128)} copy(f32[4,32]{1,0:T(4,128)} %shard_map.46) | data formatting | bytes 1024

commit v6 on v5

--- a/solution.py
+++ b/solution.py
@@ -14,49 +14,50 @@
 PLACES = {"a": (0,), "b": (1, 2), "c": (3,), "d": (4,), "e": (5, 6), "f": (7,)}
 
 PIECES = (
-    (0, 0, 0, 32, "v"),
-    (0, 0, 32, 96, "y"),
+    (0, 0, 0, 64, "v"),
+    (0, 0, 64, 64, "y"),
     (1, 0, 0, 128, "v"),
     (0, 1, 0, 128, "y"),
-    (1, 1, 0, 128, "v"),
+    (1, 1, 0, 32, "y"),
+    (1, 1, 32, 96, "v"),
 )
 
 ORDER = (
     ("s1", "o", "a", 0), ("s2", "o", "a", 0), ("v", 0, 0), ("y", 0, 0, 1), ("y", 0, 0, 2), ("ra", 0),
     ("rb", 0), ("v", 1, 0), ("y", 0, 1, 1), ("y", 0, 1, 2), ("ra", 1), ("rb", 1), ("s1", "o", "b", 0),
-    ("s3", "o", "a", 0), ("s1", "o", "d", 0), ("s2", "o", "b", 0), ("fa", 0), ("s2", "o", "d", 0), ("fb", 0),
-    ("s1", "o", "a", 1), ("v", 3, 0), ("y", 0, 3, 1), ("y", 0, 3, 2), ("x", 0, 0), ("fa", 1),
-    ("s2", "o", "a", 1), ("s1", "p", "a", 0), ("s1", "p", "b", 0), ("fb", 1), ("s1", "p", "d", 0),
-    ("y", 1, 0, 1), ("y", 1, 0, 2), ("s1", "p", "a", 1), ("y", 0, 0, 3, 1), ("y", 0, 0, 3, 2),
-    ("s2", "p", "a", 0), ("s2", "p", "b", 0), ("s2", "p", "d", 0), ("s2", "p", "a", 1), ("s3", "o", "b", 0),
-    ("y", 0, 1, 3, 1), ("v", 1, 1), ("y", 0, 1, 3, 2), ("s1", "o", "c", 0), ("s3", "o", "d", 0),
-    ("s1", "p", "c", 0), ("s3", "o", "a", 1), ("s2", "o", "c", 0), ("s3", "p", "a", 0), ("s2", "p", "c", 0),
-    ("s4", "o", "a"), ("s3", "p", "b", 0), ("v", 1, 2), ("s3", "p", "d", 0), ("s1", "o", "e", 0),
-    ("s3", "p", "a", 1), ("s1", "p", "e", 0), ("y", 0, 2, 1), ("y", 0, 2, 2), ("s1", "o", "b", 1),
-    ("s3", "o", "c", 0), ("s2", "o", "e", 0), ("x", 0, 1), ("s2", "p", "e", 0), ("s3", "p", "c", 0),
-    ("s1", "s", "a", 0), ("s1", "s", "b", 0), ("s2", "o", "b", 1), ("s1", "s", "c", 0), ("y", 0, 3, 3, 1),
-    ("y", 0, 3, 3, 2), ("s1", "s", "d", 0), ("s1", "s", "e", 0), ("s2", "s", "a", 0), ("s1", "s", "a", 1),
-    ("s2", "s", "b", 0), ("s1", "p", "b", 1), ("v", 2, 0), ("s2", "s", "c", 0), ("s1", "s", "b", 1),
-    ("s2", "s", "d", 0), ("s1", "o", "d", 1), ("s2", "s", "e", 0), ("s2", "s", "a", 1), ("s3", "o", "e", 0),
-    ("s2", "p", "b", 1), ("s1", "p", "d", 1), ("s2", "s", "b", 1), ("s3", "p", "e", 0), ("s2", "o", "d", 1),
-    ("s1", "s", "d", 1), ("s2", "p", "d", 1), ("y", 0, 4, 1), ("y", 0, 4, 2), ("s2", "s", "d", 1),
-    ("s3", "o", "b", 1), ("y", 1, 0, 3, 1), ("y", 1, 0, 3, 2), ("s3", "s", "a", 0), ("v", 3, 1),
-    ("s3", "s", "b", 0), ("s4", "o", "b"), ("y", 0, 2, 3, 1), ("y", 0, 2, 3, 2), ("s3", "s", "c", 0),
-    ("x", 1, 0), ("s3", "s", "d", 0), ("s1", "o", "c", 1), ("s3", "s", "e", 0), ("s1", "p", "c", 1),
-    ("s1", "s", "c", 1), ("s4", "p", "a"), ("s3", "s", "a", 1), ("s2", "o", "c", 1), ("s3", "p", "b", 1),
-    ("s2", "p", "c", 1), ("s2", "s", "c", 1), ("v", 3, 2), ("s3", "s", "b", 1), ("s4", "p", "b"),
-    ("s3", "o", "d", 1), ("y", 1, 2, 1), ("y", 1, 2, 2), ("s1", "o", "e", 1), ("s3", "p", "d", 1),
-    ("s1", "p", "e", 1), ("s3", "s", "d", 1), ("s1", "s", "e", 1), ("s3", "o", "c", 1), ("s2", "o", "e", 1),
-    ("y", 0, 4, 3, 1), ("y", 0, 4, 3, 2), ("s2", "p", "e", 1), ("s2", "s", "e", 1), ("s3", "p", "c", 1),
-    ("v", 4, 0), ("s3", "s", "c", 1), ("s4", "o", "d"), ("s4", "o", "c"), ("s4", "p", "c"), ("y", 1, 2, 3, 1),
-    ("y", 1, 2, 3, 2), ("s1", "o", "f", 1), ("s1", "p", "f", 1), ("x", 1, 1), ("s1", "s", "f", 1),
-    ("s4", "p", "d"), ("s3", "o", "e", 1), ("s4", "s", "a"), ("v", 1, 3), ("s2", "o", "f", 1),
-    ("s2", "p", "f", 1), ("s2", "s", "f", 1), ("s3", "p", "e", 1), ("s1", "o", "f", 0), ("s1", "p", "f", 0),
-    ("s1", "s", "f", 0), ("s4", "s", "b"), ("s3", "s", "e", 1), ("s4", "s", "c"), ("s2", "o", "f", 0),
-    ("s2", "p", "f", 0), ("s2", "s", "f", 0), ("s4", "s", "d"), ("s3", "o", "f", 1), ("y", 1, 4, 1),
-    ("y", 1, 4, 2), ("s3", "p", "f", 1), ("s4", "o", "e"), ("s3", "s", "f", 1), ("s4", "p", "e"), ("v", 3, 3),
-    ("s3", "o", "f", 0), ("s3", "p", "f", 0), ("s4", "s", "e"), ("s3", "s", "f", 0), ("y", 1, 4, 3, 1),
-    ("y", 1, 4, 3, 2), ("s4", "o", "f"), ("s4", "p", "f"), ("s4", "s", "f"),
+    ("s3", "o", "a", 0), ("s1", "o", "d", 0), ("y", 1, 0, 1), ("y", 1, 0, 2), ("fa", 0), ("s2", "o", "b", 0),
+    ("fb", 0), ("go", 1, 0), ("y", 0, 0, 3, 1), ("y", 0, 0, 3, 2), ("s2", "o", "d", 0), ("s1", "o", "a", 1),
+    ("v", 1, 1), ("x", 0, 0), ("go", 0, 1), ("y", 0, 1, 3, 1), ("y", 0, 1, 3, 2), ("fa", 1),
+    ("s1", "p", "a", 2), ("s1", "p", "b", 0), ("s1", "o", "c", 0), ("fb", 1), ("y", 1, 0, 3, 1),
+    ("y", 1, 0, 3, 2), ("s1", "p", "c", 0), ("s2", "o", "a", 1), ("s1", "p", "d", 0), ("v", 1, 2),
+    ("s1", "o", "e", 0), ("s2", "p", "a", 2), ("s2", "p", "b", 0), ("s3", "o", "b", 0), ("s1", "p", "e", 0),
+    ("s2", "o", "c", 0), ("s2", "p", "c", 0), ("s3", "o", "d", 0), ("s2", "p", "d", 0), ("s2", "o", "e", 0),
+    ("s3", "o", "a", 1), ("s2", "p", "e", 0), ("y", 0, 2, 1), ("y", 0, 2, 2), ("s3", "p", "a", 2),
+    ("s1", "o", "b", 1), ("v", 2, 0), ("s3", "p", "b", 0), ("s1", "p", "b", 1), ("s1", "o", "d", 1),
+    ("s1", "p", "d", 1), ("s3", "o", "c", 0), ("s3", "p", "c", 0), ("s2", "o", "b", 1), ("s3", "p", "d", 0),
+    ("x", 0, 1), ("go", 1, 1), ("s2", "p", "b", 1), ("s2", "o", "d", 1), ("s1", "s", "a", 2),
+    ("s2", "p", "d", 1), ("s1", "s", "b", 2), ("y", 0, 3, 1), ("y", 0, 3, 2), ("s3", "o", "e", 0),
+    ("s1", "s", "c", 0), ("s1", "s", "d", 2), ("v", 3, 0), ("s1", "s", "e", 0), ("s4", "o", "a"),
+    ("s2", "s", "a", 2), ("s3", "p", "e", 0), ("s2", "s", "b", 2), ("y", 0, 2, 3, 1), ("y", 0, 2, 3, 2),
+    ("s1", "o", "c", 1), ("s2", "s", "c", 0), ("s2", "s", "d", 2), ("s1", "p", "c", 1), ("v", 1, 3),
+    ("s2", "s", "e", 0), ("s3", "o", "b", 1), ("s1", "s", "c", 1), ("s1", "o", "f", 0), ("v", 4, 0),
+    ("s3", "p", "b", 1), ("s1", "p", "f", 0), ("s1", "s", "f", 0), ("s2", "o", "c", 1), ("s2", "p", "c", 1),
+    ("s3", "o", "d", 1), ("s2", "s", "c", 1), ("s3", "p", "d", 1), ("s2", "o", "f", 0), ("s2", "p", "f", 0),
+    ("s3", "s", "a", 2), ("s2", "s", "f", 0), ("y", 1, 2, 1), ("y", 1, 2, 2), ("s1", "o", "e", 1),
+    ("v", 5, 0), ("s1", "p", "e", 1), ("x", 1, 0), ("y", 0, 4, 1), ("y", 0, 4, 2), ("s3", "s", "b", 2),
+    ("s1", "s", "e", 1), ("s3", "s", "c", 0), ("s4", "o", "d"), ("s4", "p", "a"), ("s2", "o", "e", 1),
+    ("s3", "s", "d", 2), ("s2", "p", "e", 1), ("s4", "p", "d"), ("s3", "s", "e", 0), ("s2", "s", "e", 1),
+    ("y", 0, 5, 1), ("y", 0, 5, 2), ("s4", "o", "b"), ("v", 3, 1), ("s3", "o", "c", 1), ("s3", "p", "c", 1),
+    ("s4", "p", "b"), ("s3", "s", "c", 1), ("y", 0, 3, 3, 1), ("y", 0, 3, 3, 2), ("s3", "o", "f", 0),
+    ("s3", "p", "f", 0), ("s3", "s", "f", 0), ("y", 1, 2, 3, 1), ("y", 1, 2, 3, 2), ("s1", "o", "f", 1),
+    ("s1", "p", "f", 1), ("s1", "s", "f", 1), ("v", 3, 2), ("s3", "o", "e", 1), ("x", 1, 1), ("s4", "s", "a"),
+    ("s4", "s", "b"), ("s3", "p", "e", 1), ("v", 4, 1), ("s4", "s", "d"), ("s2", "o", "f", 1),
+    ("s2", "p", "f", 1), ("s2", "s", "f", 1), ("s3", "s", "e", 1), ("v", 4, 2), ("y", 1, 5, 1),
+    ("y", 1, 5, 2), ("s4", "o", "e"), ("y", 0, 4, 3, 1), ("y", 0, 4, 3, 2), ("s4", "p", "e"),
+    ("s4", "s", "e"), ("y", 0, 5, 3, 1), ("y", 0, 5, 3, 2), ("s3", "o", "f", 1), ("s3", "p", "f", 1),
+    ("s4", "o", "c"), ("s3", "s", "f", 1), ("s4", "p", "c"), ("s4", "s", "c"), ("y", 1, 5, 3, 1),
+    ("y", 1, 5, 3, 2), ("fold", "a", "b", "c", "d", "e"), ("v", 3, 3), ("v", 4, 3), ("s4", "ops", "f"),
+    ("fold", "f"),
 )
 
 POWER = 16
@@ -183,7 +184,7 @@
     starts, rows = {}, {}
     for event in ORDER:
         if event[0] == "s1":
-            size = len(BLOCKS[event[1]]) * len(PLACES[event[2]])
+            size = len(BLOCKS[event[1]]) * len(PLACES[event[2]]) * (1 + event[3] // 2)
             first = sum(n for _, n in starts.values())
             rows[event[1:]] = (first * seq_len + 16 * len(starts), size * seq_len + 16)
             starts[event[1:]] = (first, size)
@@ -192,18 +193,22 @@
         blocks, places, w = BLOCKS[group[0]], PLACES[group[1]], group[2]
         first, size = starts[group]
         n = len(blocks)
+        slots = range(1 + w // 2)
 
         def one(i, carry):
+            right = vals[0, places[0] + i, w] if w < 2 else vals[0, places[0] + i].reshape(2 * seq_len, -1)
             part = lax.dot_general(
                 trains[0, 2 * blocks[0] : 2 * blocks[0] + 2 * n].reshape(2 * n * seq_len, -1),
-                vals[0, places[0] + i, w],
+                right,
                 (((1,), (1,)), ((), ())),
                 preferred_element_type=jnp.float32,
             )
             for k in range(n):
                 for r in range(2):
                     at_row = (2 * k + r) * seq_len
-                    acts[r, first + i * n + k] = part[at_row : at_row + seq_len]
+                    for j in slots:
+                        unit = first + (i * n + k) * len(slots) + j
+                        acts[r, unit] = part[at_row : at_row + seq_len, j * seq_len : (j + 1) * seq_len]
             return carry
 
         lax.fori_loop(0, len(places), one, 0)
@@ -255,45 +260,55 @@
         here = whole.at[core, pl.ds(first, size)]
         send(("s3",) + group, here, here, to_core)
 
-    def grad_product(b_key, p_key):
-        blocks, places = BLOCKS[b_key], PLACES[p_key]
-        n = len(blocks)
-        for w in range(2):
-            got(("s3", b_key, p_key, w))
-
-        def one(i, carry):
-            v, b = places[0] + i // n, blocks[0] + i % n
+    def grad_product(b_keys, p_key):
+        for b_key in b_keys:
+            for w in range(3):
+                if (b_key, p_key, w) in starts:
+                    got(("s3", b_key, p_key, w))
+
+        def one(b_key, i):
+            blocks, places = BLOCKS[b_key], PLACES[p_key]
+            v, b = places[0] + i // len(blocks), blocks[0] + i % len(blocks)
             part = lax.dot_general(
                 trains[1, pl.ds(2 * b, 2)].reshape(2 * seq_len, -1),
                 vals[1, v].reshape(2 * seq_len, -1),
                 (((1,), (1,)), ((), ())),
                 preferred_element_type=jnp.float32,
             )
-            for r in range(2):
-                for w in range(2):
-                    act = whole[r, starts[b_key, p_key, w][0] + i]
+            for w in range(2):
+                if (b_key, p_key, 2) in starts:
+                    unit = starts[b_key, p_key, 2][0] + 2 * i + w
+                else:
+                    unit = starts[b_key, p_key, w][0] + i
+                for r in range(2):
                     grad = part[r * seq_len : (r + 1) * seq_len, w * seq_len : (w + 1) * seq_len]
-                    sums[v, w, b, r : r + 1] = jnp.sum(act * grad, axis=0, keepdims=True)
-            return carry
-
-        lax.fori_loop(0, n * len(places), one, 0)
+                    total = jnp.sum(whole[r, unit] * grad, axis=0, keepdims=True)
+                    sums[v, w, pl.ds(2 * b + r, 1)] = total
+
+        for b_key in b_keys:
+            count = len(BLOCKS[b_key]) * len(PLACES[p_key])
+            if len(b_keys) > 1:
+                for i in range(count):
+                    one(b_key, i)
+            else:
+                lax.fori_loop(0, count, lambda i, carry: (one(b_key, i), carry)[1], 0)
 
     group_of = ((z_lo, core), (z_lo, 1 - core), (1 - z_lo, core), (1 - z_lo, 1 - core))
 
-    def out():
-        lane = lax.broadcasted_iota(jnp.int32, (RING, 2, 128), 2)
-        scores = jnp.zeros(lane.shape, jnp.float32)
-        for v in range(2 * RING):
+    lane = lax.broadcasted_iota(jnp.int32, (8, 128), 1)
+
+    def fold(scores, p_keys):
+        for v in [v for p_key in p_keys for v in PLACES[p_key]]:
             for w in range(2):
                 its_z_hi = z_hi if w == 0 else 1 - z_hi
                 column = its_z_hi * 16 + y_at[v % RING] * 4 + (x if v < RING else twin)
-                scores = jnp.where(lane == column, jnp.sum(sums[v, w], axis=2, keepdims=True), scores)
+                scores = jnp.where(lane == column, jnp.sum(sums[v, w], axis=1, keepdims=True), scores)
+        return scores
+
+    def out(scores):
         scores = scores * (1.0 / (total_width * seq_len))
-        tiles[...] = jnp.zeros_like(tiles)
-        for b in range(RING):
-            for r in range(2):
-                at_row = (b % 2) * 2 + r
-                tiles[b // 2, at_row : at_row + 1] = scores[b, r : r + 1]
+        tiles[0, 0:4] = scores[0:4]
+        tiles[1, 0:4] = scores[4:8]
         for side, its_x in ((1, mate), (0, x)):
             for d, (its_z_lo, its_core) in enumerate(group_of):
                 if (side, d) != (0, 0):
@@ -308,7 +323,6 @@
     own_ready(0, 0)
     pass_on(0)
     pass_on(1)
-    own_ready(0, 1)
     for m in range(2):
         for h in range(2):
             send(("x", m, h), train_in[m].at[pl.ds(2 * h, 2)], trains.at[m, pl.ds(4 + 2 * h, 2)], to_mate)
@@ -316,8 +330,15 @@
         copy.wait()
 
     seen = set()
+    scores = jnp.zeros((8, 128), jnp.float32)
     for event in ORDER:
         kind = event[0]
+        if kind == "go":
+            own_ready(*event[1:])
+            continue
+        if kind == "fold":
+            scores = fold(scores, event[1:])
+            continue
         if kind == "s1":
             act_product(event[1:])
             continue
@@ -338,10 +359,7 @@
             m = event[1]
             send(("fb", m), relay.at[1, m], vals.at[m, 0, 1, half_b], to_lo)
         elif kind in ("fa", "fb"):
-            m = event[1]
-            if ("f", m) in seen:
-                own_ready(1, m)
-            seen.add(("f", m))
+            pass
         elif kind == "v":
             have(1, *event[1:])
         elif kind == "y":
@@ -352,20 +370,20 @@
             elif event[:4] in seen:
                 have(q, piece, place)
             seen.add(event[:4])
-    out()
-
-    total = tiles[0]
+    out(scores)
+
+    total = tiles[0, 0:4]
     for side in range(2):
         for d in range(4):
             if (side, d) != (0, 0):
                 got(("out", side, d))
-                total = total + arrived[side, d]
-    out_ref[...] = total[: out_ref.shape[0], : out_ref.shape[1]]
+                total = total + arrived[side, d, 0:4]
+    out_ref[...] = total[:, : out_ref.shape[1]]
     for copy in copies.values():
         copy.wait_send()
 
 
-GROUPS = 2 * len(BLOCKS) * len(PLACES)
+GROUPS = sum(1 for event in ORDER if event[0] == "s1")
 UNITS = 2 * 4 * 2 * RING
 Y_RINGS = sum(1 if first == "y" else 2 for *_, first in PIECES)
 V_COPIES = sum(RING if first == "y" else 1 for *_, first in PIECES)
@@ -392,7 +410,7 @@
             pltpu.VMEM(coded, bf16),
             pltpu.VMEM(coded, bf16),
             pltpu.VMEM((2, UNITS, seq_len, seq_len), f32),
-            pltpu.VMEM((2 * RING, 2, RING, 2, seq_len), f32),
+            pltpu.VMEM((2 * RING, 2, 8, seq_len), f32),
             pltpu.VMEM((2, 8, 128), f32),
             pltpu.VMEM((2, 4, 8, 128), f32),
             pltpu.SemaphoreType.DMA((4,)),

time: 89 us -> 84.6 us (0.951)
  Pallas kernels: 87.6 us -> 83.2 us
    pallas_call x1, Pallas kernels: 87.6 us -> 83.2 us  [per_device(): pl.pallas_call(functools.partial(kernel, width * lax.axis_size('tensor'))...]
where the time goes in v6:
time: 84.6 us; the launch traced here: 84.4 us
  Pallas kernels  83.2 us (98%)
  local copies, waits for them, and re-layouts  1.26 us (1%)
    pallas_call x1, Pallas kernels, per_device(): pl.pallas_call(functools.partial(kernel, width * lax.axis_size('tensor'))...  83.2 us

profile of v6, /device:TPU:1, one launch (start us, length us, event | category | flops | bytes accessed | tf_op | source)
XLA Modules:
  0.0 84.4 jit_solution(1779571413147672711)
XLA Ops:
  0.0 83.2 %shard_map.46 = f32[4,32]{1,0:T(4,128)} custom-call(bf16[4,128,1280]{2,1,0:T(8,128)(2,1)} %train_act.1, bf16[4,128,1280]{2,1,0:T(8,128)(2,1)} %train_grad.1, bf16[1,128,1280]{2,1,0:T(8,128)(2,1)} %val_act.1, bf16[1,128,1280]{2,1,0:T(8,128)(2,1)} %val_grad.1), custom_call_target="tpu_custom_call" | custom-call | flops 10737418240 | bytes 3300000 | tf_op jit(solution)/shard_map/pallas_call | solution.py:399
  83.2 1.3 %copy.6 = f32[4,32]{1,0:T(4,128)} copy(f32[4,32]{1,0:T(4,128)} %shard_map.46) | data formatting | bytes 1024

commit v7 on v6

--- a/solution.py
+++ b/solution.py
@@ -8,6 +8,7 @@
 from jax.sharding import PartitionSpec as P
 
 MESH = pl.DeviceIdType.MESH
+LAST = "f"
 RING = 4
 
 BLOCKS = {"o": (0, 1), "p": (2,), "s": (3,)}
@@ -17,47 +18,45 @@
     (0, 0, 0, 64, "v"),
     (0, 0, 64, 64, "y"),
     (1, 0, 0, 128, "v"),
-    (0, 1, 0, 128, "y"),
+    (0, 1, 0, 32, "y"),
+    (0, 1, 32, 96, "y"),
     (1, 1, 0, 32, "y"),
     (1, 1, 32, 96, "v"),
 )
-
+AT_ONCE = (0, 1)
+
+EARLY = (3,)
 ORDER = (
-    ("s1", "o", "a", 0), ("s2", "o", "a", 0), ("v", 0, 0), ("y", 0, 0, 1), ("y", 0, 0, 2), ("ra", 0),
-    ("rb", 0), ("v", 1, 0), ("y", 0, 1, 1), ("y", 0, 1, 2), ("ra", 1), ("rb", 1), ("s1", "o", "b", 0),
-    ("s3", "o", "a", 0), ("s1", "o", "d", 0), ("y", 1, 0, 1), ("y", 1, 0, 2), ("fa", 0), ("s2", "o", "b", 0),
-    ("fb", 0), ("go", 1, 0), ("y", 0, 0, 3, 1), ("y", 0, 0, 3, 2), ("s2", "o", "d", 0), ("s1", "o", "a", 1),
-    ("v", 1, 1), ("x", 0, 0), ("go", 0, 1), ("y", 0, 1, 3, 1), ("y", 0, 1, 3, 2), ("fa", 1),
-    ("s1", "p", "a", 2), ("s1", "p", "b", 0), ("s1", "o", "c", 0), ("fb", 1), ("y", 1, 0, 3, 1),
-    ("y", 1, 0, 3, 2), ("s1", "p", "c", 0), ("s2", "o", "a", 1), ("s1", "p", "d", 0), ("v", 1, 2),
-    ("s1", "o", "e", 0), ("s2", "p", "a", 2), ("s2", "p", "b", 0), ("s3", "o", "b", 0), ("s1", "p", "e", 0),
-    ("s2", "o", "c", 0), ("s2", "p", "c", 0), ("s3", "o", "d", 0), ("s2", "p", "d", 0), ("s2", "o", "e", 0),
-    ("s3", "o", "a", 1), ("s2", "p", "e", 0), ("y", 0, 2, 1), ("y", 0, 2, 2), ("s3", "p", "a", 2),
-    ("s1", "o", "b", 1), ("v", 2, 0), ("s3", "p", "b", 0), ("s1", "p", "b", 1), ("s1", "o", "d", 1),
-    ("s1", "p", "d", 1), ("s3", "o", "c", 0), ("s3", "p", "c", 0), ("s2", "o", "b", 1), ("s3", "p", "d", 0),
-    ("x", 0, 1), ("go", 1, 1), ("s2", "p", "b", 1), ("s2", "o", "d", 1), ("s1", "s", "a", 2),
-    ("s2", "p", "d", 1), ("s1", "s", "b", 2), ("y", 0, 3, 1), ("y", 0, 3, 2), ("s3", "o", "e", 0),
-    ("s1", "s", "c", 0), ("s1", "s", "d", 2), ("v", 3, 0), ("s1", "s", "e", 0), ("s4", "o", "a"),
-    ("s2", "s", "a", 2), ("s3", "p", "e", 0), ("s2", "s", "b", 2), ("y", 0, 2, 3, 1), ("y", 0, 2, 3, 2),
-    ("s1", "o", "c", 1), ("s2", "s", "c", 0), ("s2", "s", "d", 2), ("s1", "p", "c", 1), ("v", 1, 3),
-    ("s2", "s", "e", 0), ("s3", "o", "b", 1), ("s1", "s", "c", 1), ("s1", "o", "f", 0), ("v", 4, 0),
-    ("s3", "p", "b", 1), ("s1", "p", "f", 0), ("s1", "s", "f", 0), ("s2", "o", "c", 1), ("s2", "p", "c", 1),
-    ("s3", "o", "d", 1), ("s2", "s", "c", 1), ("s3", "p", "d", 1), ("s2", "o", "f", 0), ("s2", "p", "f", 0),
-    ("s3", "s", "a", 2), ("s2", "s", "f", 0), ("y", 1, 2, 1), ("y", 1, 2, 2), ("s1", "o", "e", 1),
-    ("v", 5, 0), ("s1", "p", "e", 1), ("x", 1, 0), ("y", 0, 4, 1), ("y", 0, 4, 2), ("s3", "s", "b", 2),
-    ("s1", "s", "e", 1), ("s3", "s", "c", 0), ("s4", "o", "d"), ("s4", "p", "a"), ("s2", "o", "e", 1),
-    ("s3", "s", "d", 2), ("s2", "p", "e", 1), ("s4", "p", "d"), ("s3", "s", "e", 0), ("s2", "s", "e", 1),
-    ("y", 0, 5, 1), ("y", 0, 5, 2), ("s4", "o", "b"), ("v", 3, 1), ("s3", "o", "c", 1), ("s3", "p", "c", 1),
-    ("s4", "p", "b"), ("s3", "s", "c", 1), ("y", 0, 3, 3, 1), ("y", 0, 3, 3, 2), ("s3", "o", "f", 0),
-    ("s3", "p", "f", 0), ("s3", "s", "f", 0), ("y", 1, 2, 3, 1), ("y", 1, 2, 3, 2), ("s1", "o", "f", 1),
-    ("s1", "p", "f", 1), ("s1", "s", "f", 1), ("v", 3, 2), ("s3", "o", "e", 1), ("x", 1, 1), ("s4", "s", "a"),
-    ("s4", "s", "b"), ("s3", "p", "e", 1), ("v", 4, 1), ("s4", "s", "d"), ("s2", "o", "f", 1),
-    ("s2", "p", "f", 1), ("s2", "s", "f", 1), ("s3", "s", "e", 1), ("v", 4, 2), ("y", 1, 5, 1),
-    ("y", 1, 5, 2), ("s4", "o", "e"), ("y", 0, 4, 3, 1), ("y", 0, 4, 3, 2), ("s4", "p", "e"),
-    ("s4", "s", "e"), ("y", 0, 5, 3, 1), ("y", 0, 5, 3, 2), ("s3", "o", "f", 1), ("s3", "p", "f", 1),
-    ("s4", "o", "c"), ("s3", "s", "f", 1), ("s4", "p", "c"), ("s4", "s", "c"), ("y", 1, 5, 3, 1),
-    ("y", 1, 5, 3, 2), ("fold", "a", "b", "c", "d", "e"), ("v", 3, 3), ("v", 4, 3), ("s4", "ops", "f"),
-    ("fold", "f"),
+    ("v", 0, 0), ("y", 0, 0, 1), ("y", 0, 0, 2), ("ra", 0), ("rb", 0), ("go", 3), ("s1", "o", "a", 0),
+    ("v", 1, 0), ("y", 0, 1, 1), ("y", 0, 1, 2), ("ra", 1), ("rb", 1), ("s1", "o", "b", 0), ("v", 3, 0),
+    ("s2", "o", "a", 0), ("s1", "o", "d", 0), ("y", 1, 0, 1), ("y", 1, 0, 2), ("fa", 0), ("fb", 0), ("go", 2),
+    ("s1", "o", "a", 1), ("s2", "o", "b", 0), ("y", 0, 0, 3, 1), ("y", 0, 0, 3, 2), ("s2", "o", "d", 0),
+    ("v", 1, 1), ("x", 0, 0), ("s1", "p", "a", 2), ("fa", 1), ("fb", 1), ("go", 5), ("y", 0, 3, 1),
+    ("y", 0, 3, 2), ("s2", "o", "a", 1), ("s1", "p", "b", 0), ("s3", "o", "a", 0), ("s1", "p", "d", 0),
+    ("y", 0, 1, 3, 1), ("y", 0, 1, 3, 2), ("s1", "op", "c", 0), ("v", 1, 2), ("s2", "p", "a", 2),
+    ("s1", "op", "e", 0), ("y", 1, 0, 3, 1), ("y", 1, 0, 3, 2), ("s2", "p", "b", 0), ("s2", "p", "d", 0),
+    ("s3", "o", "b", 0), ("s2", "op", "c", 0), ("s3", "o", "d", 0), ("s3", "o", "a", 1), ("s2", "op", "e", 0),
+    ("s3", "p", "a", 2), ("v", 2, 0), ("s1", "op", "d", 1), ("y", 0, 2, 1), ("y", 0, 2, 2),
+    ("s3", "p", "b", 0), ("s1", "op", "b", 1), ("v", 5, 0), ("y", 0, 5, 1), ("y", 0, 5, 2), ("go", 4),
+    ("y", 0, 3, 3, 1), ("y", 0, 3, 3, 2), ("v", 3, 1), ("x", 0, 1), ("s2", "op", "d", 1), ("s3", "p", "d", 0),
+    ("s3", "op", "c", 0), ("s1", "s", "a", 2), ("s1", "s", "b", 2), ("v", 3, 2), ("s1", "s", "c", 0),
+    ("s1", "s", "d", 2), ("s2", "op", "b", 1), ("s4", "o", "a"), ("s2", "s", "a", 2), ("s3", "op", "e", 0),
+    ("s2", "s", "b", 2), ("s2", "s", "c", 0), ("v", 1, 3), ("s2", "s", "d", 2), ("s3", "op", "d", 1),
+    ("y", 1, 2, 1), ("y", 1, 2, 2), ("v", 5, 1), ("s1", "s", "e", 2), ("s1", "op", "e", 1), ("v", 5, 2),
+    ("y", 0, 2, 3, 1), ("go", 6), ("y", 0, 2, 3, 2), ("s1", "ops", "c", 1), ("y", 0, 5, 3, 1),
+    ("y", 0, 5, 3, 2), ("s2", "s", "e", 2), ("s3", "op", "b", 1), ("s2", "op", "e", 1), ("s3", "s", "a", 2),
+    ("x", 1, 0), ("s4", "p", "a"), ("v", 4, 0), ("s2", "ops", "c", 1), ("s3", "s", "b", 2), ("v", 3, 3),
+    ("s3", "s", "c", 0), ("y", 0, 4, 1), ("y", 0, 4, 2), ("s3", "s", "d", 2), ("y", 1, 2, 3, 1),
+    ("y", 1, 2, 3, 2), ("s1", "o", "f", 2), ("s1", "p", "f", 2), ("s3", "s", "e", 2), ("v", 6, 0),
+    ("s1", "s", "f", 2), ("s4", "o", "d"), ("s4", "p", "d"), ("v", 5, 3), ("s2", "o", "f", 2),
+    ("s2", "p", "f", 2), ("s2", "s", "f", 2), ("s3", "op", "e", 1), ("y", 0, 6, 1), ("y", 0, 6, 2),
+    ("s4", "o", "b"), ("s4", "p", "b"), ("x", 1, 1), ("y", 0, 4, 3, 1), ("y", 0, 4, 3, 2), ("v", 4, 1),
+    ("s3", "ops", "c", 1), ("s4", "s", "a"), ("fold", "a"), ("s4", "s", "b"), ("fold", "b"), ("s4", "s", "d"),
+    ("fold", "d"), ("s3", "o", "f", 2), ("s3", "p", "f", 2), ("y", 1, 6, 1), ("y", 1, 6, 2), ("v", 4, 2),
+    ("s4", "o", "e"), ("s3", "s", "f", 2), ("s4", "p", "e"), ("y", 0, 6, 3, 1), ("y", 0, 6, 3, 2),
+    ("s4", "o", "c"), ("s4", "p", "c"), ("s4", "s", "c"), ("s4", "s", "e"), ("y", 1, 6, 3, 1), ("v", 4, 3),
+    ("y", 1, 6, 3, 2), ("fold", "c", "e"), ("s4", "ps", "f"), ("fold1", "f"), ("out", 1), ("s4", "o", "f"),
+    ("fold0", "f"), ("out", 0),
 )
 
 POWER = 16
@@ -82,6 +81,7 @@
     sums,
     tiles,
     arrived,
+    result,
     local_sem,
     send_sem,
     recv_sem,
@@ -168,11 +168,10 @@
         src = own_val(piece) if place == 0 else vals.at[m, place, w, pl.ds(row, rows)]
         send(("v", piece, place), src, vals.at[m, RING + place, w, pl.ds(row, rows)], to_twin)
 
-    def own_ready(w, m):
-        for piece, what in enumerate(PIECES):
-            if what[:2] == (w, m):
-                v_direct(piece, 0)
-                y_direct(0, piece)
+    def own_ready(piece):
+        if piece not in EARLY:
+            v_direct(piece, 0)
+        y_direct(0, piece)
 
     def have(q, piece, place):
         first = PIECES[piece][4]
@@ -181,16 +180,19 @@
         if first == "v" and q == 1 and place == 0:
             y_direct(1, piece)
 
+    def blocks_of(keys):
+        return [b for key in keys for b in BLOCKS[key]]
+
     starts, rows = {}, {}
     for event in ORDER:
         if event[0] == "s1":
-            size = len(BLOCKS[event[1]]) * len(PLACES[event[2]]) * (1 + event[3] // 2)
+            size = len(blocks_of(event[1])) * len(PLACES[event[2]]) * (1 + event[3] // 2)
             first = sum(n for _, n in starts.values())
             rows[event[1:]] = (first * seq_len + 16 * len(starts), size * seq_len + 16)
             starts[event[1:]] = (first, size)
 
     def act_product(group):
-        blocks, places, w = BLOCKS[group[0]], PLACES[group[1]], group[2]
+        blocks, places, w = blocks_of(group[0]), PLACES[group[1]], group[2]
         first, size = starts[group]
         n = len(blocks)
         slots = range(1 + w // 2)
@@ -260,11 +262,19 @@
         here = whole.at[core, pl.ds(first, size)]
         send(("s3",) + group, here, here, to_core)
 
+    arrived_acts = set()
+
     def grad_product(b_keys, p_key):
+        acts_of = {}
         for b_key in b_keys:
-            for w in range(3):
-                if (b_key, p_key, w) in starts:
-                    got(("s3", b_key, p_key, w))
+            for group in starts:
+                if b_key in group[0] and p_key == group[1]:
+                    if group not in arrived_acts:
+                        arrived_acts.add(group)
+                        got(("s3",) + group)
+                    for w in range(2):
+                        if group[2] in (w, 2):
+                            acts_of[b_key, w] = group
 
         def one(b_key, i):
             blocks, places = BLOCKS[b_key], PLACES[p_key]
@@ -276,18 +286,20 @@
                 preferred_element_type=jnp.float32,
             )
             for w in range(2):
-                if (b_key, p_key, 2) in starts:
-                    unit = starts[b_key, p_key, 2][0] + 2 * i + w
-                else:
-                    unit = starts[b_key, p_key, w][0] + i
+                group = acts_of[b_key, w]
+                in_group = blocks_of(group[0])
+                unit = i // len(blocks) * len(in_group) + b - in_group[0]
+                if group[2] == 2:
+                    unit = 2 * unit + w
+                unit = starts[group][0] + unit
                 for r in range(2):
                     grad = part[r * seq_len : (r + 1) * seq_len, w * seq_len : (w + 1) * seq_len]
                     total = jnp.sum(whole[r, unit] * grad, axis=0, keepdims=True)
-                    sums[v, w, pl.ds(2 * b + r, 1)] = total
+                    sums[b // 2, v, w, pl.ds(2 * (b % 2) + r, 1)] = total
 
         for b_key in b_keys:
             count = len(BLOCKS[b_key]) * len(PLACES[p_key])
-            if len(b_keys) > 1:
+            if p_key == LAST:
                 for i in range(count):
                     one(b_key, i)
             else:
@@ -295,34 +307,35 @@
 
     group_of = ((z_lo, core), (z_lo, 1 - core), (1 - z_lo, core), (1 - z_lo, 1 - core))
 
-    lane = lax.broadcasted_iota(jnp.int32, (8, 128), 1)
-
-    def fold(scores, p_keys):
+    lane = lax.broadcasted_iota(jnp.int32, (4, 128), 1)
+
+    def fold(side, p_keys):
         for v in [v for p_key in p_keys for v in PLACES[p_key]]:
             for w in range(2):
                 its_z_hi = z_hi if w == 0 else 1 - z_hi
                 column = its_z_hi * 16 + y_at[v % RING] * 4 + (x if v < RING else twin)
-                scores = jnp.where(lane == column, jnp.sum(sums[v, w], axis=1, keepdims=True), scores)
-        return scores
-
-    def out(scores):
-        scores = scores * (1.0 / (total_width * seq_len))
-        tiles[0, 0:4] = scores[0:4]
-        tiles[1, 0:4] = scores[4:8]
-        for side, its_x in ((1, mate), (0, x)):
-            for d, (its_z_lo, its_core) in enumerate(group_of):
-                if (side, d) != (0, 0):
-                    device = at(z_hi, y, its_x, its_z_lo, its_core)
-                    send(("out", side, d), tiles.at[side], arrived.at[side, d], device)
+                total = jnp.sum(sums[side, v, w], axis=1, keepdims=True)
+                scores[side] = jnp.where(lane == column, total, scores[side])
+
+    def out(side):
+        tiles[side, 0:4] = scores[side] * (1.0 / (total_width * seq_len))
+        for d in (3, 2, 1, 0):
+            its_z_lo, its_core = group_of[d]
+            if (side, d) != (0, 0):
+                device = at(z_hi, y, (x, mate)[side], its_z_lo, its_core)
+                send(("out", side, d), tiles.at[side], arrived.at[side, d], device)
 
     half_a, half_b = pl.ds(0, seq_len // 2), pl.ds(seq_len // 2, seq_len // 2)
     def pass_on(m):
         send(("ra", m), val_in[m].at[0, half_a], relay.at[0, m], to_lo)
         send(("rb", m), val_in[m].at[0, half_b], relay.at[1, m], to_hi)
 
-    own_ready(0, 0)
-    pass_on(0)
-    pass_on(1)
+    for piece in AT_ONCE:
+        own_ready(piece)
+    for m in range(2):
+        pass_on(m)
+    for piece in EARLY:
+        v_direct(piece, 0)
     for m in range(2):
         for h in range(2):
             send(("x", m, h), train_in[m].at[pl.ds(2 * h, 2)], trains.at[m, pl.ds(4 + 2 * h, 2)], to_mate)
@@ -330,14 +343,19 @@
         copy.wait()
 
     seen = set()
-    scores = jnp.zeros((8, 128), jnp.float32)
+    scores = [jnp.zeros((4, 128), jnp.float32)] * 2
     for event in ORDER:
         kind = event[0]
         if kind == "go":
             own_ready(*event[1:])
             continue
-        if kind == "fold":
-            scores = fold(scores, event[1:])
+        if kind.startswith("fold"):
+            for side in range(2):
+                if kind != ("fold1", "fold0")[side]:
+                    fold(side, event[1:])
+            continue
+        if kind == "out":
+            out(event[1])
             continue
         if kind == "s1":
             act_product(event[1:])
@@ -358,8 +376,6 @@
         elif kind == "rb":
             m = event[1]
             send(("fb", m), relay.at[1, m], vals.at[m, 0, 1, half_b], to_lo)
-        elif kind in ("fa", "fb"):
-            pass
         elif kind == "v":
             have(1, *event[1:])
         elif kind == "y":
@@ -370,17 +386,18 @@
             elif event[:4] in seen:
                 have(q, piece, place)
             seen.add(event[:4])
-    out(scores)
-
     total = tiles[0, 0:4]
     for side in range(2):
         for d in range(4):
             if (side, d) != (0, 0):
                 got(("out", side, d))
                 total = total + arrived[side, d, 0:4]
-    out_ref[...] = total[:, : out_ref.shape[1]]
+    result[...] = total[:, : out_ref.shape[1]]
+    copy_out = pltpu.make_async_copy(result, out_ref, local_sem.at[0])
+    copy_out.start()
     for copy in copies.values():
         copy.wait_send()
+    copy_out.wait()
 
 
 GROUPS = sum(1 for event in ORDER if event[0] == "s1")
@@ -400,7 +417,7 @@
         functools.partial(kernel, width * lax.axis_size("tensor")),
         out_shape=jax.ShapeDtypeStruct((n_train, n_val), f32),
         in_specs=[anywhere] * 4,
-        out_specs=pl.BlockSpec(memory_space=pltpu.VMEM),
+        out_specs=anywhere,
         scratch_shapes=[
             pltpu.VMEM((2, 2 * n_train, seq_len, width), bf16),
             pltpu.VMEM((2, 2 * RING, 2, seq_len, width), bf16),
@@ -410,9 +427,10 @@
             pltpu.VMEM(coded, bf16),
             pltpu.VMEM(coded, bf16),
             pltpu.VMEM((2, UNITS, seq_len, seq_len), f32),
-            pltpu.VMEM((2 * RING, 2, 8, seq_len), f32),
+            pltpu.VMEM((2, 2 * RING, 2, 4, seq_len), f32),
             pltpu.VMEM((2, 8, 128), f32),
             pltpu.VMEM((2, 4, 8, 128), f32),
+            pltpu.VMEM((n_train, n_val), f32),
             pltpu.SemaphoreType.DMA((4,)),
             pltpu.SemaphoreType.DMA((N_COPIES,)),
             pltpu.SemaphoreType.DMA((N_COPIES,)),

time: 84.6 us -> 83.9 us (level)
  no operation moved by 1% of the time
where the time goes in v7:
time: 83.9 us; the launch traced here: 83.8 us
  Pallas kernels  82.5 us (98%)
  local copies, waits for them, and re-layouts  1.26 us (2%)
    pallas_call x1, Pallas kernels, per_device(): pl.pallas_call(functools.partial(kernel, width * lax.axis_size('tensor'))...  82.5 us

profile of v7, /device:TPU:1, one launch (start us, length us, event | category | flops | bytes accessed | tf_op | source)
XLA Modules:
  0.0 83.8 jit_solution(15325280636578149995)
XLA Ops:
  0.0 82.5 %shard_map.46 = f32[4,32]{1,0:T(4,128)} custom-call(bf16[4,128,1280]{2,1,0:T(8,128)(2,1)} %train_act.1, bf16[4,128,1280]{2,1,0:T(8,128)(2,1)} %train_grad.1, bf16[1,128,1280]{2,1,0:T(8,128)(2,1)} %val_act.1, bf16[1,128,1280]{2,1,0:T(8,128)(2,1)} %val_grad.1), custom_call_target="tpu_custom_call" | custom-call | flops 10737418240 | bytes 3300000 | tf_op jit(solution)/shard_map/pallas_call | solution.py:416
  82.5 1.3 %copy.6 = f32[4,32]{1,0:T(4,128)} copy(f32[4,32]{1,0:T(4,128)} %shard_map.46) | data formatting | bytes 1024

commit v8 on v7

--- a/solution.py
+++ b/solution.py
@@ -279,12 +279,18 @@
         def one(b_key, i):
             blocks, places = BLOCKS[b_key], PLACES[p_key]
             v, b = places[0] + i // len(blocks), blocks[0] + i % len(blocks)
-            part = lax.dot_general(
-                trains[1, pl.ds(2 * b, 2)].reshape(2 * seq_len, -1),
+            add_up(b_key, i, v, b, grads(2 * b, 2, v))
+
+        def grads(train, count, v):
+            return lax.dot_general(
+                trains[1, pl.ds(train, count)].reshape(count * seq_len, -1),
                 vals[1, v].reshape(2 * seq_len, -1),
                 (((1,), (1,)), ((), ())),
                 preferred_element_type=jnp.float32,
             )
+
+        def add_up(b_key, i, v, b, part):
+            blocks = BLOCKS[b_key]
             for w in range(2):
                 group = acts_of[b_key, w]
                 in_group = blocks_of(group[0])
@@ -297,13 +303,17 @@
                     total = jnp.sum(whole[r, unit] * grad, axis=0, keepdims=True)
                     sums[b // 2, v, w, pl.ds(2 * (b % 2) + r, 1)] = total
 
+        if p_key == LAST and len(blocks_of(b_keys)) == 2:
+            (v,), first = PLACES[p_key], blocks_of(b_keys)[0]
+            part = grads(2 * first, 4, v)
+            for b_key in b_keys:
+                for i, b in enumerate(BLOCKS[b_key]):
+                    row = (b - first) * 2 * seq_len
+                    add_up(b_key, i, v, b, part[row : row + 2 * seq_len])
+            return
         for b_key in b_keys:
             count = len(BLOCKS[b_key]) * len(PLACES[p_key])
-            if p_key == LAST:
-                for i in range(count):
-                    one(b_key, i)
-            else:
-                lax.fori_loop(0, count, lambda i, carry: (one(b_key, i), carry)[1], 0)
+            lax.fori_loop(0, count, lambda i, carry: (one(b_key, i), carry)[1], 0)
 
     group_of = ((z_lo, core), (z_lo, 1 - core), (1 - z_lo, core), (1 - z_lo, 1 - core))
 

time: 83.9 us -> 84.5 us (level)
  no operation moved by 1% of the time
where the time goes in v8:
time: 84.5 us; the launch traced here: 84.4 us
  Pallas kernels  83.1 us (98%)
  local copies, waits for them, and re-layouts  1.26 us (1%)
    pallas_call x1, Pallas kernels, per_device(): pl.pallas_call(functools.partial(kernel, width * lax.axis_size('tensor'))...  83.1 us

profile of v8, /device:TPU:1, one launch (start us, length us, event | category | flops | bytes accessed | tf_op | source)
XLA Modules:
  0.0 84.4 jit_solution(17135078089611551832)
XLA Ops:
  0.0 83.1 %shard_map.46 = f32[4,32]{1,0:T(4,128)} custom-call(bf16[4,128,1280]{2,1,0:T(8,128)(2,1)} %train_act.1, bf16[4,128,1280]{2,1,0:T(8,128)(2,1)} %train_grad.1, bf16[1,128,1280]{2,1,0:T(8,128)(2,1)} %val_act.1, bf16[1,128,1280]{2,1,0:T(8,128)(2,1)} %val_grad.1), custom_call_target="tpu_custom_call" | custom-call | flops 10737418240 | bytes 3300000 | tf_op jit(solution)/shard_map/pallas_call | solution.py:426
  83.1 1.3 %copy.6 = f32[4,32]{1,0:T(4,128)} copy(f32[4,32]{1,0:T(4,128)} %shard_map.46) | data formatting | bytes 1024

commit v9 on v7

--- a/solution.py
+++ b/solution.py
@@ -330,10 +330,10 @@
         send(("ra", m), val_in[m].at[0, half_a], relay.at[0, m], to_lo)
         send(("rb", m), val_in[m].at[0, half_b], relay.at[1, m], to_hi)
 
+    pass_on(0)
     for piece in AT_ONCE:
         own_ready(piece)
-    for m in range(2):
-        pass_on(m)
+    pass_on(1)
     for piece in EARLY:
         v_direct(piece, 0)
     for m in range(2):

time: 83.9 us -> 83.9 us (level)
  no operation moved by 1% of the time
where the time goes in v9:
time: 83.9 us; the launch traced here: 83.8 us
  Pallas kernels  82.5 us (98%)
  local copies, waits for them, and re-layouts  1.26 us (2%)
    pallas_call x1, Pallas kernels, per_device(): pl.pallas_call(functools.partial(kernel, width * lax.axis_size('tensor'))...  82.5 us

profile of v9, /device:TPU:1, one launch (start us, length us, event | category | flops | bytes accessed | tf_op | source)
XLA Modules:
  0.0 83.8 jit_solution(13522899173100561917)
XLA Ops:
  0.0 82.5 %shard_map.46 = f32[4,32]{1,0:T(4,128)} custom-call(bf16[4,128,1280]{2,1,0:T(8,128)(2,1)} %train_act.1, bf16[4,128,1280]{2,1,0:T(8,128)(2,1)} %train_grad.1, bf16[1,128,1280]{2,1,0:T(8,128)(2,1)} %val_act.1, bf16[1,128,1280]{2,1,0:T(8,128)(2,1)} %val_grad.1), custom_call_target="tpu_custom_call" | custom-call | flops 10737418240 | bytes 3300000 | tf_op jit(solution)/shard_map/pallas_call | solution.py:416
  82.6 1.3 %copy.6 = f32[4,32]{1,0:T(4,128)} copy(f32[4,32]{1,0:T(4,128)} %shard_map.46) | data formatting | bytes 1024
